TPU v7x, 256 devices: a whole 4x4x8 slice. The times are simulated.
256 devices in a mesh: role: 2 (over z_hi), dp: 16 (over z_lo, y), tensor: 8 (over x, core).
Axes of the slice: x: 4, y: 4, z: 8 (z_hi: 2, z_lo: 4; z = z_hi * 4 + z_lo), core: 2. Of those that a mesh axis runs over, the one named last changes fastest.
Arguments:
- kv_weight: bfloat16 [2048, 8192], P(('role', 'dp'), 'tensor'), may hold values from -0.0625 to 0.0625
- kv_bias: bfloat16 [2048], P('tensor'), may hold values from -3 to 3
- norm_gain: bfloat16 [8192], P('tensor'), may hold values from 0.099609375 to 1.8984375
- page_states: bfloat16 [65536, 8192], P(('role', 'dp'), 'tensor'), may hold values from -1800 to 1800
- page_replica: int32 [512, 1], P(('role', 'dp')), may hold values from 0 to 15; in each aligned block of 16 rows (0 to 15, 16 to 31, ...) at most 2 rows name the same one
- page_pos: int32 [512], P(('role', 'dp')), may hold values from 0 to 255
- page_fill: int32 [512], P(('role', 'dp')), may hold values from 1 to 128
- learn_normed: bfloat16 [8192, 8192], P(('role', 'dp'), 'tensor'), may hold values from -6 to 6
- learn_cot: bfloat16 [8192, 2048], P(('role', 'dp')), may hold values from -2.5 to 2.5
Outputs:
- kv_cache: bfloat16 [1024, 128, 2048], P(('role', 'dp'), None, 'tensor')
- normed_grad: bfloat16 [8192, 8192], P(('role', 'dp'), 'tensor')
- weight_grad: float32 [2048, 8192], P(('role', 'dp'), 'tensor')
Inputs may be any that keep to these rules, and one draw needn't show every extreme that they name: `page_replica`: within the 16 pages of one device, at most 2 name the same replica.
All inputs are finite; a program needn't handle non-finite values.
Results may differ from a plain program's by a relative error of at most 0.022.
Values may be sent and summed in bfloat16 or wider, within the bound.
No kernel may reach another device: no remote copies, remote signals or barrier semaphores. Data moves between devices by JAX's collectives and lax.ppermute only.
A program may use at most 128 MiB of HBM per device.

v0:
```python
import jax
import jax.numpy as jnp
from jax import lax
from jax.sharding import PartitionSpec as P

HD = 128


EPSILON = 1e-06
ROPE_BASE = 1000000.0


def rotate_keys(fresh_kv, positions):
    head_size = fresh_kv.shape[-1]
    half_size = head_size // 2
    exponent = jnp.arange(half_size, dtype=jnp.float32) * (2.0 / head_size)
    frequency = jnp.power(jnp.float32(ROPE_BASE), -exponent)
    angles = positions.astype(jnp.float32)[:, None] * frequency[None, :]
    cosine = jnp.cos(angles)[:, None, :]
    sine_part = jnp.sin(angles)[:, None, :]
    key_part = fresh_kv[:, :, 0, :]
    first_half = key_part[..., :half_size]
    second_half = key_part[..., half_size:]
    turned = jnp.concatenate(
        [
            first_half * cosine - second_half * sine_part,
            second_half * cosine + first_half * sine_part,
        ],
        axis=-1,
    )
    return jnp.stack([turned, fresh_kv[:, :, 1, :]], axis=2)


def shards(
    kv_weight,
    kv_bias,
    norm_gain,
    page_states,
    page_replica,
    page_pos,
    page_fill,
    learn_normed,
    learn_cot,
):
    weight_rows = lax.all_gather(kv_weight, ("role", "dp"), axis=0, tiled=True)
    normed_grad = jnp.dot(learn_cot, weight_rows, preferred_element_type=jnp.float32).astype(
        jnp.bfloat16
    )
    weight_grad = lax.psum_scatter(
        lax.dot_general(
            learn_cot, learn_normed, (((0,), (0,)), ((), ())), preferred_element_type=jnp.float32
        ).astype(jnp.bfloat16),
        ("role", "dp"),
        scatter_dimension=0,
        tiled=True,
    ).astype(jnp.float32)
    token_rows = page_states.shape[0]
    page_count = page_fill.shape[0]
    page_len = token_rows // page_count
    feature_count = norm_gain.shape[0] * lax.axis_size("tensor")
    widened = page_states.astype(jnp.float32)
    scaled = (widened * norm_gain.astype(jnp.float32)[None, :]).astype(jnp.bfloat16)
    partial_sums = lax.dot_general(
        scaled, weight_rows, (((1,), (1,)), ((), ())), preferred_element_type=jnp.float32
    )
    head_part = lax.psum_scatter(
        partial_sums.astype(jnp.bfloat16), "tensor", scatter_dimension=1, tiled=True
    ).astype(jnp.float32)
    row_squares = lax.psum(jnp.sum(widened * widened, axis=1), "tensor")
    fresh_kv = (
        head_part * lax.rsqrt(row_squares / feature_count + EPSILON)[:, None]
        + kv_bias.astype(jnp.float32)[None, :]
    )
    head_size = HD
    head_count = head_part.shape[1] // (2 * head_size)
    offsets = jnp.arange(page_len, dtype=jnp.int32)
    positions = (page_pos[:, None] * page_len + offsets[None, :]).reshape(-1)
    turned = rotate_keys(fresh_kv.reshape(token_rows, head_count, 2, head_size), positions)
    live_rows = (offsets[None, :] < page_fill[:, None]).reshape(-1)
    kv_pages = jnp.where(live_rows[:, None], turned.reshape(token_rows, -1), 0.0).astype(
        jnp.bfloat16
    )
    replicas = lax.axis_size("dp")
    capacity = max(2, 2 * page_count // replicas)
    slot_count = replicas * capacity
    owners = page_replica[:, 0]
    same_owner = owners[:, None] == owners[None, :]
    earlier = jnp.arange(page_count)[None, :] < jnp.arange(page_count)[:, None]
    page_rank = jnp.sum(jnp.where(same_owner & earlier, 1, 0), axis=1).astype(jnp.int32)
    target = owners * capacity + page_rank
    chooser = (target[None, :] == jnp.arange(slot_count, dtype=jnp.int32)[:, None]).astype(
        jnp.bfloat16
    )
    flattened = kv_pages.reshape(page_count, -1)
    outgoing = jnp.dot(chooser, flattened, preferred_element_type=jnp.float32).astype(jnp.bfloat16)
    outgoing = outgoing.reshape(slot_count, page_len, -1)
    kv_cache = lax.all_to_all(outgoing, "dp", split_axis=0, concat_axis=0, tiled=True)
    return (kv_cache, normed_grad, weight_grad)


def solution(mesh):
    placed = (
        P(("role", "dp"), "tensor"),
        P("tensor"),
        P("tensor"),
        P(("role", "dp"), "tensor"),
        P(("role", "dp"), None),
        P(("role", "dp")),
        P(("role", "dp")),
        P(("role", "dp"), "tensor"),
        P(("role", "dp"), None),
    )
    return jax.shard_map(
        shards,
        mesh=mesh,
        in_specs=placed,
        out_specs=(
            P(("role", "dp"), None, "tensor"),
            P(("role", "dp"), "tensor"),
            P(("role", "dp"), "tensor"),
        ),
        check_vma=False,
    )
```

profile of v0, /device:TPU:32, one launch (start us, length us, event | category | flops | bytes accessed | tf_op | source)
XLA Modules:
  0.0 413.6 jit_solution(120797573963024106)
XLA Ops:
  7.2 0.0 copy-start
  7.2 0.0 all-gather.2.cloned.1.call-start
  7.2 0.7 all-gather.2.cloned.1.call-update
  7.9 0.0 reduce-scatter.3.cloned.1.call-start
  8.0 0.7 convert_element_type.46
  8.6 86.6 %all-gather.2.cloned.1.call-done = bf16[2048,1024]{1,0:T(8,128)(2,1)} async-done(((bf16[64,1024]{1,0:T(8,128)(2,1)}), bf16[2048,1024]{1,0:T(8,128)(2,1)}) %all-gather.2.cloned.1.call-update) | async-done | bytes 4194320 | tf_op jit(solution)/shard_map/all_gather | solution.py:45
  95.3 13.9 %convolution_convert_fusion.1 = bf16[2048,2048]{1,0:T(8,128)(2,1)} fusion(bf16[2048,1024]{1,0:T(8,128)(2,1)} %all-gather.2.cloned.1.call-done, bf16[2048,1024]{1,0:T(8,128)(2,1)} %param.12, f32[1024]{0:T(1024)S(1)} %convert_element_type.46), kind=kOutput, calls=%fused_computation.5 | convolution fusion | flops 8600420352 | bytes 16781312 | tf_op jit(solution)/shard_map/dot_general | solution.py:63
  109.2 0.0 copy-start.1
  109.2 0.0 reduce-scatter.3.cloned.1.call-update
  109.2 0.0 reduce-scatter.5.cloned.1.call-start
  109.3 0.0 copy-done
  109.3 1.0 copy-done.1
  110.2 3.2 convolution_convert_fusion.2
  113.4 0.0 copy-start.3
  113.4 0.0 copy-start.2
  113.5 0.0 copy-start.5
  113.5 0.0 copy-start.4
  113.5 0.0 reduce-scatter.5.cloned.1.call-update
  113.5 0.6 copy-done.3
  114.1 0.0 copy-done.2
  114.1 0.1 iota_compare_fusion.2
  114.2 0.4 broadcast_in_dim.22
  114.6 1.3 copy.15
  115.9 3.4 fusion.1
  119.3 13.4 %psum.7 = f32[2048]{0:T(1024)S(1)} all-reduce(f32[2048]{0:T(1024)S(1)} %fusion.1), channel_id=1, replica_groups=mesh['role'=2,'dp'=16,'tensor'=8] {'tensor'}, use_global_device_ids=true, to_apply=%region_3.0 | all-reduce | flops 2048 | bytes 16384 | tf_op jit(solution)/shard_map/psum | solution.py:69
  132.7 0.0 copy-done.5
  132.7 0.2 select_reduce_fusion
  132.9 0.0 copy-done.4
  132.9 0.1 convert_bitcast_fusion
  133.0 28.7 %reduce-scatter.3.cloned.1.call-done = bf16[2048,256]{1,0:T(8,128)(2,1)} async-done(((bf16[2048,2048]{1,0:T(8,128)(2,1)}), bf16[2048,256]{1,0:T(8,128)(2,1)}) %reduce-scatter.3.cloned.1.call-update) | async-done | bytes 1048592 | tf_op jit(solution)/shard_map/reduce_scatter | solution.py:66
  161.7 1.6 multiply_add_fusion
  163.3 2.1 reshape.148
  165.3 2.0 slice.16
  167.3 2.3 slice.19
  169.7 4.5 %fusion.8 = (f32[2048,1,64]{2,0,1:T(8,128)S(1)}, f32[2048,1,64]{2,0,1:T(8,128)S(1)}) fusion(f32[2048,1,128]{2,0,1:T(8,128)S(1)} %bitcast.19, f32[64]{0:T(128)S(1)} %negate_power_fusion, f32[2048]{0:T(1024)S(1)} %convert_bitcast_fusion), kind=kLoop, calls=%fused_computation.18 | loop fusion | flops 917504 | bytes 2105600 | tf_op jit(solution)/shard_map/sub | solution.py:26
  174.2 0.3 pad_maximum_fusion.1
  174.5 2.1 pad_maximum_fusion
  176.6 0.8 reshape.149
  177.5 1.7 convolution_convert_fusion
  179.2 1.8 copy.16
  181.0 7.7 %all-to-all-start = ((bf16[32,128,256]{2,1,0:T(8,128)(2,1)}), bf16[32,128,256]{2,1,0:T(8,128)(2,1)S(1)}, u32[]{:S(2)}, u32[]{:S(2)}) async-start(bf16[32,128,256]{2,1,0:T(8,128)(2,1)} %bitcast.20), calls=%async_computation.1 | async-start | bytes 4194304 | tf_op jit(solution)/shard_map/all_to_all | solution.py:97
  188.7 4.3 %convolution_convert_fusion.3 = bf16[256,1024]{1,0:T(8,128)(2,1)} fusion(bf16[256,2048]{1,0:T(8,128)(2,1)S(1)} %copy-done, bf16[2048,1024]{1,0:T(8,128)(2,1)} %all-gather.2.cloned.1.call-done), kind=kOutput, calls=%fused_computation.17 | convolution fusion | flops 1074003968 | bytes 5767168 | tf_op jit(solution)/shard_map/dot_general | solution.py:46
  193.0 211.1 %reduce-scatter.5.cloned.1.call-done = bf16[64,1024]{1,0:T(8,128)(2,1)} async-done(((bf16[2048,1024]{1,0:T(8,128)(2,1)}), bf16[64,1024]{1,0:T(8,128)(2,1)}) %reduce-scatter.5.cloned.1.call-update) | async-done | bytes 131088 | tf_op jit(solution)/shard_map/reduce_scatter | solution.py:49
  404.1 1.6 convert_element_type.57
  405.7 0.0 all-to-all-done
  405.7 1.3 copy.18
  (5 shorter events, 0.0 us)
Async XLA Ops:
  7.2 102.1 %copy-start = (bf16[256,2048]{1,0:T(8,128)(2,1)S(1)}, bf16[256,2048]{1,0:T(8,128)(2,1)}, u32[]{:S(2)}) copy-start(bf16[256,2048]{1,0:T(8,128)(2,1)} %param.17) | copy-start | bytes 3145732
  7.2 88.1 %all-gather.2.cloned.1.call-start = ((), (), s32[]{:S(2)}) async-start(), calls=%async_computation.3 | async-start | bytes 4325376 | tf_op jit(solution)/shard_map/all_gather | solution.py:45
  7.9 153.8 %reduce-scatter.3.cloned.1.call-start = ((), (), s32[]{:S(2)}) async-start(), calls=%async_computation.4 | async-start | bytes 9437184 | tf_op jit(solution)/shard_map/reduce_scatter | solution.py:66
  109.2 1.0 copy-start.1
  109.2 294.9 %reduce-scatter.5.cloned.1.call-start = ((), (), s32[]{:S(2)}) async-start(), calls=%async_computation.5 | async-start | bytes 4325376 | tf_op jit(solution)/shard_map/reduce_scatter | solution.py:49
  113.4 0.7 copy-start.3
  113.4 0.7 copy-start.2
  113.5 19.2 %copy-start.5 = (s32[16,1]{0,1:T(1,128)S(1)}, s32[16,1]{0,1:T(1,128)}, u32[]{:S(2)}) copy-start(s32[16,1]{0,1:T(1,128)} %param.13) | copy-start | bytes 196
  113.5 19.4 %copy-start.4 = (s32[16]{0:T(128)S(1)}, s32[16]{0:T(128)}, u32[]{:S(2)}) copy-start(s32[16]{0:T(128)} %param.14) | copy-start | bytes 196
  181.0 224.7 %all-to-all-start = ((bf16[32,128,256]{2,1,0:T(8,128)(2,1)}), bf16[32,128,256]{2,1,0:T(8,128)(2,1)S(1)}, u32[]{:S(2)}, u32[]{:S(2)}) async-start(bf16[32,128,256]{2,1,0:T(8,128)(2,1)} %bitcast.20), calls=%async_computation.1 | async-start | bytes 4194304 | tf_op jit(solution)/shard_map/all_to_all | solution.py:97
Sparse Core Ops, SparseCore 0:
  10.6 84.6 all-gather.1
  109.3 52.3 reduce-scatter.2
  165.6 238.4 reduce-scatter.4
where the time goes:
time: 415 us; the launch traced here: 414 us
  waiting for transfers between devices  327 us (79%)
  matrix products  23.1 us (6%)
  other arithmetic  14.6 us (4%)
  between operations  13.9 us (3%)
  local copies, waits for them, and re-layouts  13.7 us (3%)
  blocking collectives  13.4 us (3%)
  starting transfers between devices  7.85 us (2%)
    reduce_scatter x1, waiting for transfers between devices, shards(): lax.psum_scatter(lax.dot_general(learn_cot, learn_normed, (((0,), (0,)),...  211 us
    all_gather x1, waiting for transfers between devices, shards(): weight_rows = lax.all_gather(kv_weight, ('role', 'dp'), axis=0, tiled=True)  86.6 us
    reduce_scatter x1, waiting for transfers between devices, shards(): lax.psum_scatter(partial_sums.astype(jnp.bfloat16), 'tensor', scatter_dim...  28.7 us
    dot_general x1, matrix products, shards(): lax.dot_general(scaled, weight_rows, (((1,), (1,)), ((), ())), preferred_...  13.9 us
    psum x1, blocking collectives, shards(): row_squares = lax.psum(jnp.sum(widened * widened, axis=1), 'tensor')  13.4 us
  transfers between devices with their start and end apart: 4, of which 3 were waited for; matrix products, arithmetic and copies ran while one was open for 8% of the time, Pallas kernels for 0%

commit v1 on v0

v1 whole, which is shorter than its diff:
```python
import jax
import jax.numpy as jnp
from jax import lax
from jax.experimental import pallas as pl
from jax.experimental.pallas import tpu as pltpu
from jax.sharding import Mesh, PartitionSpec as P

HD = 128
PAGE = 128
EPSILON = 1e-06
ROPE_BASE = 1000000.0

Z = ("role", "zl")
ROWS = ("role", "zl", "y")
DP = ("zl", "y")
TENSOR = ("x", "core")

CHUNKS = ((0, 64), (64, 64))
F32 = jnp.float32
BF16 = jnp.bfloat16


def ring(size, step):
    return [(i, (i + step) % size) for i in range(size)]


def shift(value, axis, size, step):
    return lax.ppermute(value, axis, ring(size, step))


def after(value, *earlier):
    return lax.optimization_barrier((value, earlier))[0]


def by_index(blocks, index):
    size = len(blocks)
    twice = jnp.stack(blocks + blocks[:-1])
    return lax.dynamic_slice_in_dim(twice, (size - index) % size, size, 0)


def unwritten(shape, dtype):
    return pl.pallas_call(
        lambda out_ref: None,
        out_specs=pl.BlockSpec(memory_space=pl.ANY),
        out_shape=jax.ShapeDtypeStruct(shape, dtype),
    )()


def gather_weight(weight):
    ny, y = lax.axis_size("y"), lax.axis_index("y")
    line = by_index([weight] + [shift(weight, "y", ny, -s) for s in range(1, ny)], y)
    line = line.reshape(-1, weight.shape[1])
    return lax.all_gather(line, Z, axis=0, tiled=False), line


def dot_rows(scaled_ref, weight_ref, rows):
    return lax.dot_general(
        scaled_ref[...].reshape(rows, scaled_ref.shape[2]), weight_ref[0], (((1,), (1,)), ((), ())),
        preferred_element_type=F32,
    )


def project_kernel(place_ref, scaled_ref, weight_ref, out_ref):
    out_ref[0] = dot_rows(scaled_ref, weight_ref, out_ref.shape[1]).astype(BF16)


def project_add_kernel(place_ref, scaled_ref, weight_ref, other_ref, *out_refs):
    rows = other_ref.shape[1]
    total = dot_rows(scaled_ref, weight_ref, rows) + other_ref[0].astype(F32)
    for step, out_ref in enumerate(out_refs):
        @pl.when(pl.program_id(0) == step)
        def _(out_ref=out_ref):
            out_ref[...] = total.astype(BF16)


def project(scaled, weight, place, chunk, other=None):
    pages, page, depth = scaled.shape
    heads, cols, _ = weight.shape
    heads //= 2
    start, part = chunk
    rows = pages * part

    def head(h, place_ref):
        return lax.rem(place_ref[0] + h, heads)

    specs = [
        pl.BlockSpec((pages, part, depth), lambda h, place_ref: (0, start // part, 0)),
        pl.BlockSpec((1, cols, depth), lambda h, place_ref: (2 * head(h, place_ref) + place_ref[1], 0, 0)),
    ]
    args = [scaled, weight]
    if other is None:
        out_specs = pl.BlockSpec((1, rows, cols), lambda h, place_ref: (head(h, place_ref), 0, 0))
        out_shape = jax.ShapeDtypeStruct((heads, rows, cols), BF16)
    else:
        specs.append(pl.BlockSpec((1, rows, cols), lambda h, place_ref: (head(h, place_ref), 0, 0)))
        args.append(other)
        out_specs = [pl.BlockSpec((rows, cols), lambda h, place_ref: (0, 0))] * heads
        out_shape = [jax.ShapeDtypeStruct((rows, cols), BF16)] * heads
    return pl.pallas_call(
        project_kernel if other is None else project_add_kernel,
        grid_spec=pltpu.PrefetchScalarGridSpec(
            num_scalar_prefetch=1, grid=(heads,), in_specs=specs, out_specs=out_specs
        ),
        out_shape=out_shape,
        compiler_params=pltpu.CompilerParams(vmem_limit_bytes=24 * 2**20),
        cost_estimate=pl.CostEstimate(
            flops=2 * rows * depth * cols * heads,
            bytes_accessed=2 * (rows * depth + heads * cols * (depth + rows)),
            transcendentals=0,
        ),
    )(place, *args)


def finish(parts, inverse, cosine, sine, bias, target, fill, chunk, slots):
    sources = len(parts)
    pages, part, cols = parts[0].shape
    group = 4
    start = chunk[0]

    def kernel(target_ref, fill_ref, inverse_ref, cosine_ref, sine_ref, bias_ref, *refs):
        part_refs, out_ref = refs[:-1], refs[-1]
        step = pl.program_id(0)

        @pl.when(step == 0)
        def _():
            out_ref[...] = jnp.zeros_like(out_ref)

        bias_row = bias_ref[...].astype(F32)
        offset = lax.broadcasted_iota(jnp.int32, (part, HD), 0) + start
        for i in range(group):
            page = step * group + i
            total = part_refs[0][i].astype(F32)
            for part_ref in part_refs[1:]:
                total = total + part_ref[i].astype(F32)
            scale = inverse_ref[i]
            key = total[:, :HD] * scale + bias_row[:, :HD]
            value = total[:, HD:] * scale + bias_row[:, HD:]
            key = key * cosine_ref[i] + pltpu.roll(key, HD // 2, 1) * sine_ref[i]
            live = offset < fill_ref[page]
            where = target_ref[page]
            out_ref[where, :, :HD] = jnp.where(live, key, 0.0).astype(BF16)
            out_ref[where, :, HD:] = jnp.where(live, value, 0.0).astype(BF16)

    table = pl.BlockSpec((group, part, HD), lambda g, *_: (g, start // part, 0))
    return pl.pallas_call(
        kernel,
        grid_spec=pltpu.PrefetchScalarGridSpec(
            num_scalar_prefetch=2,
            grid=(pages // group,),
            in_specs=[
                table,
                table,
                table,
                pl.BlockSpec((1, cols), lambda g, *_: (0, 0)),
            ]
            + [pl.BlockSpec((group, part, cols), lambda g, *_: (g, 0, 0))] * sources,
            out_specs=pl.BlockSpec((slots, part, cols), lambda g, *_: (0, 0, 0)),
        ),
        out_shape=jax.ShapeDtypeStruct((slots, part, cols), BF16),
        compiler_params=pltpu.CompilerParams(vmem_limit_bytes=48 * 2**20),
        cost_estimate=pl.CostEstimate(
            flops=12 * pages * part * cols,
            bytes_accessed=2 * part * cols * (sources * pages + slots) + 12 * pages * part * HD,
            transcendentals=0,
        ),
    )(target, fill, inverse, cosine, sine, bias, *parts)


def shards(
    kv_weight,
    kv_bias,
    norm_gain,
    page_states,
    page_replica,
    page_pos,
    page_fill,
    learn_normed,
    learn_cot,
):
    nz, ny, nx = lax.axis_size(Z), lax.axis_size("y"), lax.axis_size("x")
    core, x, y, z = (lax.axis_index(name) for name in ("core", "x", "y", Z))
    pages = page_fill.shape[0]
    depth = page_states.shape[1]
    feature_count = depth * lax.axis_size(TENSOR)
    rows = kv_weight.shape[0]

    tokens = learn_cot.shape[0]
    half = HD // 2
    replicas = lax.axis_size(DP)
    capacity = max(2, 2 * pages // replicas)
    slots = replicas * capacity

    weight, line = gather_weight(kv_weight)

    cot = after(learn_cot, line).reshape(tokens, nz, ny, rows).transpose(0, 2, 1, 3)
    terms = lax.dot_general(
        cot.reshape(tokens, -1), learn_normed, (((0,), (0,)), ((), ())), preferred_element_type=F32
    ).astype(BF16)
    terms = lax.psum_scatter(terms, "y", scatter_dimension=0, tiled=True)

    states, gain, place, owners = after(
        (page_states, norm_gain, page_pos, page_replica[:, 0]), line
    )
    widened = states.astype(F32)
    scaled = (widened * gain.astype(F32)[None, :]).astype(BF16).reshape(pages, PAGE, depth)
    squares = jnp.sum(widened * widened, axis=1).reshape(pages, PAGE)
    squares = squares + shift(squares, "core", 2, 1)
    squares = squares + shift(squares, "x", nx, 1) + shift(squares, "x", nx, 2) + shift(squares, "x", nx, 3)
    inverse = lax.rsqrt(squares / feature_count + EPSILON)
    inverse = jnp.broadcast_to(inverse[:, :, None], (pages, PAGE, HD))

    exponent = jnp.arange(half, dtype=F32) * (2.0 / HD)
    frequency = jnp.power(F32(ROPE_BASE), -exponent)
    positions = place[:, None] * PAGE + jnp.arange(PAGE, dtype=jnp.int32)[None, :]
    angles = positions.astype(F32)[:, :, None] * frequency[None, None, :]
    cosine, sine = jnp.cos(angles), jnp.sin(angles)
    cosine = jnp.concatenate([cosine, cosine], axis=2)
    sine = jnp.concatenate([-sine, sine], axis=2)

    earlier = jnp.arange(pages)[None, :] < jnp.arange(pages)[:, None]
    same = owners[:, None] == owners[None, :]
    rank = jnp.sum(jnp.where(same & earlier, 1, 0), axis=1).astype(jnp.int32)
    target = owners * capacity + rank

    weight, scaled, inverse, cosine, sine, target = lax.optimization_barrier(
        (weight, scaled, inverse, cosine, sine, target)
    )
    weight_grad = lax.psum_scatter(terms, Z, scatter_dimension=0, tiled=True).astype(F32)

    own, far = jnp.stack([x, core]), jnp.stack([x, 1 - core])
    mine = []
    away = [shift(project(scaled, weight, far, chunk), "core", 2, 1) for chunk in CHUNKS[:2]]
    for c, chunk in enumerate(CHUNKS):
        mine.append(project(scaled, weight, own, chunk, away[c]))
        if c + 2 < len(CHUNKS):
            scaled = after(scaled, mine[c])
            away.append(shift(project(scaled, weight, far, CHUNKS[c + 2]), "core", 2, 1))

    kv_cache = unwritten((slots, PAGE, 2 * HD), BF16)
    for c, chunk in enumerate(CHUNKS):
        start, part = chunk
        parts = [m if s == 0 else shift(m, "x", nx, s) for s, m in enumerate(mine[c])]
        parts = [p.reshape(pages, part, 2 * HD) for p in parts]
        placed = finish(
            parts, inverse, cosine, sine, kv_bias[None, :], target, page_fill, chunk, slots
        )
        if c == 0:
            placed = after(placed, mine[-1], weight_grad)
        else:
            placed = after(placed, piece)
        piece = lax.all_to_all(placed, DP, 0, 0, tiled=True)
        kv_cache = lax.dynamic_update_slice(kv_cache, piece, (0, start, 0))

    learn_cot, _ = lax.optimization_barrier((learn_cot, placed))
    normed_grad = jnp.dot(
        learn_cot, weight.reshape(-1, depth), preferred_element_type=F32
    ).astype(BF16)
    return (kv_cache, normed_grad, weight_grad)


def solution(mesh):
    ny = 4
    nz = mesh.shape["dp"] // ny
    nx = mesh.shape["tensor"] // 2
    torus = Mesh(
        mesh.devices.reshape(mesh.shape["role"], nz, ny, nx, 2), ("role", "zl", "y", "x", "core")
    )
    placed = (
        P(ROWS, TENSOR),
        P(TENSOR),
        P(TENSOR),
        P(ROWS, TENSOR),
        P(ROWS, None),
        P(ROWS),
        P(ROWS),
        P(ROWS, TENSOR),
        P(ROWS, None),
    )
    return jax.shard_map(
        shards,
        mesh=torus,
        in_specs=placed,
        out_specs=(P(ROWS, None, TENSOR), P(ROWS, TENSOR), P(ROWS, TENSOR)),
        check_vma=False,
    )
```

time: 415 us -> 215 us (0.52)
  waiting for transfers between devices: 327 us -> 91.1 us
  starting transfers between devices: 7.85 us -> 38.6 us
  Pallas kernels: 0 us -> 25.6 us
  matrix products: 23.1 us -> 7.49 us
  blocking collectives: 13.4 us -> 0 us
  local copies, waits for them, and re-layouts: 13.7 us -> 21.7 us
    reduce_scatter x2, waiting for transfers between devices: 240 us -> 0.01 us  [the longest x1 0.01 us: shards(): terms = lax.psum_scatter(terms, 'y', scatter_dimension=0, tiled=True)]
    all_gather x1, waiting for transfers between devices: 86.6 us -> 30.2 us  [gather_weight(): return (lax.all_gather(line, Z, axis=0, tiled=False), line)]
    ppermute x0 -> x15, waiting for transfers between devices: none -> 42.8 us  [shift(): return lax.ppermute(value, axis, ring(size, step))]
    pallas_call x0 -> x7, Pallas kernels: none -> 25.6 us  [the longest x4 19.5 us: project(): pl.pallas_call(project_kernel if other is None else project_add_kernel, g...]
    ppermute x0 -> x15, starting transfers between devices: none -> 21.9 us  [shift(): return lax.ppermute(value, axis, ring(size, step))]
    all_to_all x1 -> x2, waiting for transfers between devices: 0.01 us -> 18 us  [shards(): piece = lax.all_to_all(placed, DP, 0, 0, tiled=True)]
    dot_general x4 -> x2, matrix products: 23.1 us -> 7.49 us  [the longest x1 4.23 us: shards(): jnp.dot(learn_cot, weight.reshape(-1, depth), preferred_element_type=F32)]
    psum x1 -> x0, blocking collectives: 13.4 us -> none  [shards(): row_squares = lax.psum(jnp.sum(widened * widened, axis=1), 'tensor')]
  transfers between devices with their start and end apart: 4 -> 20, of which waited for: 3 -> 10; matrix products, arithmetic and copies ran while one was open for 8% -> 11% of each run, Pallas kernels for 0% -> 12%
where the time goes in v1:
time: 215 us; the launch traced here: 213 us
  waiting for transfers between devices  91.1 us (42%)
  starting transfers between devices  38.6 us (18%)
  Pallas kernels  25.6 us (12%)
  local copies, waits for them, and re-layouts  21.7 us (10%)
  between operations  15.7 us (7%)
  other arithmetic  12.9 us (6%)
  matrix products  7.49 us (3%)
    ppermute x15, waiting for transfers between devices, shift(): return lax.ppermute(value, axis, ring(size, step))  42.8 us
    all_gather x1, waiting for transfers between devices, gather_weight(): return (lax.all_gather(line, Z, axis=0, tiled=False), line)  30.2 us
    ppermute x15, starting transfers between devices, shift(): return lax.ppermute(value, axis, ring(size, step))  21.9 us
    pallas_call x4, Pallas kernels, project(): pl.pallas_call(project_kernel if other is None else project_add_kernel, g...  19.5 us
    all_to_all x2, waiting for transfers between devices, shards(): piece = lax.all_to_all(placed, DP, 0, 0, tiled=True)  18 us
    all_to_all x2, starting transfers between devices, shards(): piece = lax.all_to_all(placed, DP, 0, 0, tiled=True)  16.5 us
    unnamed x38, local copies, waits for them, and re-layouts  15.6 us
    pallas_call x2, Pallas kernels, finish(): pl.pallas_call(kernel, grid_spec=pltpu.PrefetchScalarGridSpec(num_scalar_...  6.03 us
  transfers between devices with their start and end apart: 20, of which 10 were waited for; matrix products, arithmetic and copies ran while one was open for 11% of the time, Pallas kernels for 12%

profile of v1, /device:TPU:32, one launch (start us, length us, event | category | flops | bytes accessed | tf_op | source)
XLA Modules:
  0.0 212.9 jit_solution(14336522842888949700)
XLA Ops:
  8.1 3.1 %collective-permute-start = (bf16[64,1024]{1,0:T(8,128)(2,1)}, bf16[64,1024]{1,0:T(8,128)(2,1)S(1)}, u32[]{:S(2)}, u32[]{:S(2)}) collective-permute-start(bf16[64,1024]{1,0:T(8,128)(2,1)} %param.9), channel_id=1, source_target_pairs={{0,24},{8,0},{16,8},{24,16},{1,25},{9,1},{17,9},{25,17},{2,26},{10... | collective-permute-start | bytes 393224 | tf_op jit(solution)/shard_map/ppermute | solution.py:28
  11.8 1.0 collective-permute-start.2
  12.8 0.9 bitcast_dynamic-update-slice_fusion.5
  13.7 3.3 %collective-permute-done = bf16[64,1024]{1,0:T(8,128)(2,1)S(1)} collective-permute-done((bf16[64,1024]{1,0:T(8,128)(2,1)}, bf16[64,1024]{1,0:T(8,128)(2,1)S(1)}, u32[]{:S(2)}, u32[]{:S(2)}) %collective-permute-start) | collective-permute-done | bytes 131104 | tf_op jit(solution)/shard_map/ppermute | solution.py:28
  17.0 2.2 %collective-permute-done.1 = bf16[64,1024]{1,0:T(8,128)(2,1)S(1)} collective-permute-done((bf16[64,1024]{1,0:T(8,128)(2,1)}, bf16[64,1024]{1,0:T(8,128)(2,1)S(1)}, u32[]{:S(2)}, u32[]{:S(2)}) %collective-permute-start.1) | collective-permute-done | bytes 131104 | tf_op jit(solution)/shard_map/ppermute | solution.py:28
  19.2 1.4 collective-permute-done.2
  20.6 0.9 bitcast_dynamic-update-slice_fusion.6
  21.6 0.8 constant_dynamic-slice_fusion
  22.5 1.5 copy.16
  24.1 3.3 %convolution_convert_fusion = bf16[2048,1024]{1,0:T(8,128)(2,1)} fusion(bf16[256,2048]{0,1:T(8,128)(2,1)S(1)} %bitcast.52, bf16[256,1024]{1,0:T(8,128)(2,1)S(1)} %copy-done), kind=kOutput, calls=%fused_computation.4 | convolution fusion | flops 1075838976 | bytes 5767168 | tf_op jit(solution)/shard_map/dot_general | solution.py:196
  28.0 5.5 %fusion.1 = (f32[2048]{0:T(1024)S(1)}, bf16[2048,1024]{1,0:T(8,128)(2,1)}) fusion(bf16[2048,1024]{1,0:T(8,128)(2,1)} %param.12, f32[1024]{0:T(1024)S(1)} %convert_element_type.26), kind=kLoop, calls=%fused_computation.3 | loop fusion | flops 10483712 | bytes 8400896 | tf_op jit(solution)/shard_map/reduce_sum | solution.py:206
  33.8 3.7 %fusion.2 = (f32[16,128,64]{2,1,0:T(8,128)S(1)}, f32[16,128,64]{2,1,0:T(8,128)S(1)}, f32[16,128,64]{2,1,0:T(8,128)S(1)}) fusion(f32[64]{0:T(128)S(1)} %negate_power_fusion, f32[16,128]{1,0:T(8,128)S(1)} %add_convert_fusion), kind=kLoop, calls=%fused_computation.10 | loop fusion | flops 262144 | bytes 1581312 | tf_op jit(solution)/shard_map/neg | solution.py:218
  37.5 1.6 collective-permute-start.4
  39.1 2.7 %collective-permute-start.5 = (f32[16,128]{1,0:T(8,128)S(1)}, f32[16,128]{1,0:T(8,128)S(1)}, u32[]{:S(2)}, u32[]{:S(2)}) collective-permute-start(f32[16,128]{1,0:T(8,128)S(1)} %bitcast_add_fusion), channel_id=1, source_target_pairs={{0,4},{2,6},{4,0},{6,2},{1,5},{3,7},{5,1},{7,3},{8,12},{10,14},{12... | collective-permute-start | bytes 24584 | tf_op jit(solution)/shard_map/ppermute | solution.py:28
  41.8 1.4 collective-permute-start.6
  43.3 1.6 pad_maximum_fusion
  45.5 30.2 %all-gather.2.cloned.1.call-done.weight_ref = bf16[8,256,1024]{2,1,0:T(8,128)(2,1)} async-done(((bf16[1,256,1024]{2,1,0:T(8,128)(2,1)}), bf16[8,256,1024]{2,1,0:T(8,128)(2,1)}) %all-gather.2.cloned.1.call-update) | async-done | bytes 4194320 | tf_op jit(solution)/shard_map/all_gather | solution.py:53
  76.0 2.3 %copy-done.1 = bf16[2048,1024]{1,0:T(8,128)(2,1)S(1)} copy-done((bf16[2048,1024]{1,0:T(8,128)(2,1)S(1)}, bf16[2048,1024]{1,0:T(8,128)(2,1)}, u32[]{:S(2)}) %copy-start.1) | copy-done | bytes 4194328
  78.3 2.2 %copy-done.3 = bf16[8,256,1024]{2,1,0:T(8,128)(2,1)S(1)} copy-done((bf16[8,256,1024]{2,1,0:T(8,128)(2,1)S(1)}, bf16[8,256,1024]{2,1,0:T(8,128)(2,1)}, u32[]{:S(2)}) %copy-start.3) | copy-done | bytes 4194328
  80.5 4.6 %shard_map.113 = bf16[4,1024,256]{2,1,0:T(8,128)(2,1)} custom-call(s32[2]{0:T(128)S(1)} %pad_add_fusion.1.place_ref, bf16[16,128,1024]{2,1,0:T(8,128)(2,1)S(1)} %bitcast.39, bf16[8,256,1024]{2,1,0:T(8,128)(2,1)S(1)} %copy-done.3), custom_call_target="tpu_custom_call" | custom-call | flops 2147483648 | bytes 6291456 | tf_op jit(solution)/shard_map/pallas_call | solution.py:99
  85.1 4.6 %shard_map.116 = bf16[4,1024,256]{2,1,0:T(8,128)(2,1)} custom-call(s32[2]{0:T(128)S(1)} %pad_add_fusion.1.place_ref, bf16[16,128,1024]{2,1,0:T(8,128)(2,1)S(1)} %bitcast.40, bf16[8,256,1024]{2,1,0:T(8,128)(2,1)S(1)} %copy-done.3), custom_call_target="tpu_custom_call" | custom-call | flops 2147483648 | bytes 6291456 | tf_op jit(solution)/shard_map/pallas_call | solution.py:99
  90.3 2.2 %copy-done.2 = bf16[2048,1024]{1,0:T(8,128)(2,1)S(1)} copy-done((bf16[2048,1024]{1,0:T(8,128)(2,1)S(1)}, bf16[2048,1024]{1,0:T(8,128)(2,1)}, u32[]{:S(2)}) %copy-start.2) | copy-done | bytes 4194328
  92.5 2.2 %copy-done.4 = bf16[8,256,1024]{2,1,0:T(8,128)(2,1)S(1)} copy-done((bf16[8,256,1024]{2,1,0:T(8,128)(2,1)S(1)}, bf16[8,256,1024]{2,1,0:T(8,128)(2,1)}, u32[]{:S(2)}) %copy-start.4) | copy-done | bytes 4194328
  94.6 5.2 %shard_map.114 = (bf16[1024,256]{1,0:T(8,128)(2,1)S(1)}, bf16[1024,256]{1,0:T(8,128)(2,1)S(1)}, bf16[1024,256]{1,0:T(8,128)(2,1)S(1)}, bf16[1024,256]{1,0:T(8,128)(2,1)S(1)}) custom-call(s32[2]{0:T(128)S(1)} %pad_add_fusion.place_ref, bf16[16,128,1024]{2,1,0:T(8,128)(2,1)S(1)} %bitcast.41, bf16[8,256,1024]{2,1,0:T(8,128)(2,1)S(1)} %copy-done.4, ...), custom_call_target="tpu_custom_call" | custom-call | flops 2147483648 | bytes 6291456 | tf_op jit(solution)/shard_map/pallas_call | solution.py:99
  99.8 1.5 collective-permute-start.8
  101.4 2.7 %collective-permute-start.9 = (bf16[1024,256]{1,0:T(8,128)(2,1)S(1)}, bf16[1024,256]{1,0:T(8,128)(2,1)S(1)}, u32[]{:S(2)}, u32[]{:S(2)}) collective-permute-start(bf16[1024,256]{1,0:T(8,128)(2,1)S(1)} %get-tuple-element.37), channel_id=1, source_target_pairs={{0,4},{2,6},{4,0},{6,2},{1,5},{3,7},{5,1},{7,3},{8,12},{10,14},{12... | collective-permute-start | bytes 1572872 | tf_op jit(solution)/shard_map/ppermute | solution.py:28
  104.1 1.4 collective-permute-start.10
  105.5 5.2 %shard_map.117 = (bf16[1024,256]{1,0:T(8,128)(2,1)S(1)}, bf16[1024,256]{1,0:T(8,128)(2,1)S(1)}, bf16[1024,256]{1,0:T(8,128)(2,1)S(1)}, bf16[1024,256]{1,0:T(8,128)(2,1)S(1)}) custom-call(s32[2]{0:T(128)S(1)} %pad_add_fusion.place_ref, bf16[16,128,1024]{2,1,0:T(8,128)(2,1)S(1)} %bitcast.42, bf16[8,256,1024]{2,1,0:T(8,128)(2,1)S(1)} %copy-done.4, ...), custom_call_target="tpu_custom_call" | custom-call | flops 2147483648 | bytes 6291456 | tf_op jit(solution)/shard_map/pallas_call | solution.py:99
  111.5 0.8 copy-done.9
  112.3 0.8 copy-done.10
  113.1 2.0 collective-permute-done.8
  115.1 12.0 %collective-permute-done.9 = bf16[1024,256]{1,0:T(8,128)(2,1)S(1)} collective-permute-done((bf16[1024,256]{1,0:T(8,128)(2,1)S(1)}, bf16[1024,256]{1,0:T(8,128)(2,1)S(1)}, u32[]{:S(2)}, u32[]{:S(2)}) %collective-permute-start.9) | collective-permute-done | bytes 524320 | tf_op jit(solution)/shard_map/ppermute | solution.py:28
  127.1 3.0 %shard_map.115 = bf16[32,64,256]{2,1,0:T(8,128)(2,1)S(1)} custom-call(s32[16]{0:T(128)S(1)} %multiply_add_fusion.target_ref, s32[16]{0:T(128)S(1)} %copy-done.7, f32[16,128,128]{2,1,0:T(8,128)S(1)} %broadcast_in_dim.10.inverse_ref, f32[16,128,128]{2,1,0:T(8,128)S(1)} %get-tuple-element.31.cosine_ref, f32[16,128,128]{2,1,0:T(8,128)} %get-tuple-element.32.sine_ref, ...), custom_call_target="tpu_custom_call" | custom-call | flops 3145728 | bytes 4718592 | tf_op jit(solution)/shard_map/pallas_call | solution.py:145
  130.1 1.0 copy-done.5
  131.1 1.6 convert_element_type.30
  132.7 8.9 %all-to-all-start = ((bf16[32,64,256]{2,1,0:T(8,128)(2,1)}), bf16[32,64,256]{2,1,0:T(8,128)(2,1)}, u32[]{:S(2)}, u32[]{:S(2)}) async-start(bf16[32,64,256]{2,1,0:T(8,128)(2,1)} %copy-done.5), calls=%async_computation.2 | async-start | bytes 2097152 | tf_op jit(solution)/shard_map/all_to_all | solution.py:251
  141.6 1.4 collective-permute-start.12
  143.0 2.4 %collective-permute-start.13 = (bf16[1024,256]{1,0:T(8,128)(2,1)}, bf16[1024,256]{1,0:T(8,128)(2,1)S(1)}, u32[]{:S(2)}, u32[]{:S(2)}) collective-permute-start(bf16[1024,256]{1,0:T(8,128)(2,1)} %copy-done.9), channel_id=1, source_target_pairs={{0,4},{2,6},{4,0},{6,2},{1,5},{3,7},{5,1},{7,3},{8,12},{10,14},{12... | collective-permute-start | bytes 1572872 | tf_op jit(solution)/shard_map/ppermute | solution.py:28
  145.4 1.5 collective-permute-start.14
  146.9 9.2 %collective-permute-done.12 = bf16[1024,256]{1,0:T(8,128)(2,1)S(1)} collective-permute-done((bf16[1024,256]{1,0:T(8,128)(2,1)}, bf16[1024,256]{1,0:T(8,128)(2,1)S(1)}, u32[]{:S(2)}, u32[]{:S(2)}) %collective-permute-start.12) | collective-permute-done | bytes 524320 | tf_op jit(solution)/shard_map/ppermute | solution.py:28
  156.1 12.1 %collective-permute-done.13 = bf16[1024,256]{1,0:T(8,128)(2,1)S(1)} collective-permute-done((bf16[1024,256]{1,0:T(8,128)(2,1)}, bf16[1024,256]{1,0:T(8,128)(2,1)S(1)}, u32[]{:S(2)}, u32[]{:S(2)}) %collective-permute-start.13) | collective-permute-done | bytes 524320 | tf_op jit(solution)/shard_map/ppermute | solution.py:28
  168.2 3.0 %shard_map.118 = bf16[32,64,256]{2,1,0:T(8,128)(2,1)S(1)} custom-call(s32[16]{0:T(128)S(1)} %multiply_add_fusion.target_ref, s32[16]{0:T(128)S(1)} %copy-done.7, f32[16,128,128]{2,1,0:T(8,128)S(1)} %broadcast_in_dim.10.inverse_ref, f32[16,128,128]{2,1,0:T(8,128)S(1)} %get-tuple-element.31.cosine_ref, f32[16,128,128]{2,1,0:T(8,128)} %get-tuple-element.32.sine_ref, ...), custom_call_target="tpu_custom_call" | custom-call | flops 3145728 | bytes 4718592 | tf_op jit(solution)/shard_map/pallas_call | solution.py:145
  171.2 1.0 copy-done.6
  172.2 7.7 %all-to-all-start.1 = ((bf16[32,64,256]{2,1,0:T(8,128)(2,1)}), bf16[32,64,256]{2,1,0:T(8,128)(2,1)S(1)}, u32[]{:S(2)}, u32[]{:S(2)}) async-start(bf16[32,64,256]{2,1,0:T(8,128)(2,1)} %copy-done.6), calls=%async_computation.3 | async-start | bytes 2097152 | tf_op jit(solution)/shard_map/all_to_all | solution.py:251
  179.9 2.3 %constant_dynamic-update-slice_fusion.1 = bf16[32,128,256]{2,1,0:T(8,128)(2,1)} fusion(bf16[32,128,256]{2,1,0:T(8,128)(2,1)} %shard_map.112, bf16[32,64,256]{2,1,0:T(8,128)(2,1)} %all-to-all-done), kind=kLoop, calls=%fused_computation.24 | loop fusion | bytes 2097152 | tf_op jit(solution)/shard_map/dynamic_update_slice | solution.py:252
  182.2 4.2 %convolution_convert_fusion.1 = bf16[256,1024]{1,0:T(8,128)(2,1)} fusion(bf16[256,2048]{1,0:T(8,128)(2,1)S(1)} %copy-done.11, bf16[2048,1024]{1,0:T(8,128)(2,1)} %bitcast.43), kind=kOutput, calls=%fused_computation.7 | convolution fusion | flops 1074003968 | bytes 5767168 | tf_op jit(solution)/shard_map/dot_general | solution.py:255
  186.4 18.0 %all-to-all-done.1 = bf16[32,64,256]{2,1,0:T(8,128)(2,1)S(1)} async-done(((bf16[32,64,256]{2,1,0:T(8,128)(2,1)}), bf16[32,64,256]{2,1,0:T(8,128)(2,1)S(1)}, u32[]{:S(2)}, u32[]{:S(2)}) %all-to-all-start.1) | async-done | bytes 1048608 | tf_op jit(solution)/shard_map/all_to_all | solution.py:251
  204.5 1.0 constant_dynamic-update-slice_fusion
  (64 shorter events, 4.2 us)
Async XLA Ops:
  8.0 16.1 %copy-start = (bf16[256,1024]{1,0:T(8,128)(2,1)S(1)}, bf16[256,1024]{1,0:T(8,128)(2,1)}, u32[]{:S(2)}) copy-start(bf16[256,1024]{1,0:T(8,128)(2,1)} %param.16) | copy-start | bytes 1572868
  8.0 67.7 %all-gather.2.cloned.1.call-start = ((), (), s32[]{:S(2)}) async-start(), calls=%async_computation.4 | async-start | bytes 4718592 | tf_op jit(solution)/shard_map/all_gather | solution.py:53
  8.1 9.0 %collective-permute-start = (bf16[64,1024]{1,0:T(8,128)(2,1)}, bf16[64,1024]{1,0:T(8,128)(2,1)S(1)}, u32[]{:S(2)}, u32[]{:S(2)}) collective-permute-start(bf16[64,1024]{1,0:T(8,128)(2,1)} %param.9), channel_id=1, source_target_pairs={{0,24},{8,0},{16,8},{24,16},{1,25},{9,1},{17,9},{25,17},{2,26},{10... | collective-permute-start | bytes 393224 | tf_op jit(solution)/shard_map/ppermute | solution.py:28
  11.1 8.1 %collective-permute-start.1 = (bf16[64,1024]{1,0:T(8,128)(2,1)}, bf16[64,1024]{1,0:T(8,128)(2,1)S(1)}, u32[]{:S(2)}, u32[]{:S(2)}) collective-permute-start(bf16[64,1024]{1,0:T(8,128)(2,1)} %param.9), channel_id=1, source_target_pairs={{0,16},{8,24},{16,0},{24,8},{1,17},{9,25},{17,1},{25,9},{2,18},{10... | collective-permute-start | bytes 393224 | tf_op jit(solution)/shard_map/ppermute | solution.py:28
  11.8 8.8 %collective-permute-start.2 = (bf16[64,1024]{1,0:T(8,128)(2,1)}, bf16[64,1024]{1,0:T(8,128)(2,1)S(1)}, u32[]{:S(2)}, u32[]{:S(2)}) collective-permute-start(bf16[64,1024]{1,0:T(8,128)(2,1)} %param.9), channel_id=1, source_target_pairs={{0,8},{8,16},{16,24},{24,0},{1,9},{9,17},{17,25},{25,1},{2,10},{10... | collective-permute-start | bytes 393224 | tf_op jit(solution)/shard_map/ppermute | solution.py:28
  22.5 67.7 %reduce-scatter.3.cloned.1.call-start = ((), (), s32[]{:S(2)}) async-start(), calls=%async_computation.5 | async-start | bytes 5242880 | tf_op jit(solution)/shard_map/reduce_scatter | solution.py:199
  27.3 0.7 copy-start.12
  27.4 103.7 %reduce-scatter.5.cloned.1.call-start = ((), (), s32[]{:S(2)}) async-start(), calls=%async_computation.6 | async-start | bytes 1179648 | tf_op jit(solution)/shard_map/reduce_scatter | solution.py:228
  28.0 5.5 %copy-start.14 = (s32[16,1]{0,1:T(1,128)S(1)}, s32[16,1]{0,1:T(1,128)}, u32[]{:S(2)}) copy-start(s32[16,1]{0,1:T(1,128)} %param.13) | copy-start | bytes 196
  28.0 5.6 %copy-start.13 = (s32[16]{0:T(128)S(1)}, s32[16]{0:T(128)}, u32[]{:S(2)}) copy-start(s32[16]{0:T(128)} %param.14) | copy-start | bytes 196
  33.5 4.0 %collective-permute-start.3 = (f32[16,128]{1,0:T(8,128)S(1)}, f32[16,128]{1,0:T(8,128)S(1)}, u32[]{:S(2)}, u32[]{:S(2)}) collective-permute-start(f32[16,128]{1,0:T(8,128)S(1)} %bitcast.55), channel_id=1, source_target_pairs={{0,1},{1,0},{2,3},{3,2},{4,5},{5,4},{6,7},{7,6},{8,9},{9,8},{10,11... | collective-permute-start | bytes 24584 | tf_op jit(solution)/shard_map/ppermute | solution.py:28
  37.5 7.4 %collective-permute-start.4 = (f32[16,128]{1,0:T(8,128)S(1)}, f32[16,128]{1,0:T(8,128)S(1)}, u32[]{:S(2)}, u32[]{:S(2)}) collective-permute-start(f32[16,128]{1,0:T(8,128)S(1)} %bitcast_add_fusion), channel_id=1, source_target_pairs={{0,2},{2,4},{4,6},{6,0},{1,3},{3,5},{5,7},{7,1},{8,10},{10,12},{12... | collective-permute-start | bytes 24584 | tf_op jit(solution)/shard_map/ppermute | solution.py:28
  39.1 5.8 %collective-permute-start.5 = (f32[16,128]{1,0:T(8,128)S(1)}, f32[16,128]{1,0:T(8,128)S(1)}, u32[]{:S(2)}, u32[]{:S(2)}) collective-permute-start(f32[16,128]{1,0:T(8,128)S(1)} %bitcast_add_fusion), channel_id=1, source_target_pairs={{0,4},{2,6},{4,0},{6,2},{1,5},{3,7},{5,1},{7,3},{8,12},{10,14},{12... | collective-permute-start | bytes 24584 | tf_op jit(solution)/shard_map/ppermute | solution.py:28
  41.8 3.7 %collective-permute-start.6 = (f32[16,128]{1,0:T(8,128)S(1)}, f32[16,128]{1,0:T(8,128)S(1)}, u32[]{:S(2)}, u32[]{:S(2)}) collective-permute-start(f32[16,128]{1,0:T(8,128)S(1)} %bitcast_add_fusion), channel_id=1, source_target_pairs={{0,6},{2,0},{4,2},{6,4},{1,7},{3,1},{5,3},{7,5},{8,14},{10,8},{12,... | collective-permute-start | bytes 24584 | tf_op jit(solution)/shard_map/ppermute | solution.py:28
  76.0 2.3 %copy-start.1 = (bf16[2048,1024]{1,0:T(8,128)(2,1)S(1)}, bf16[2048,1024]{1,0:T(8,128)(2,1)}, u32[]{:S(2)}) copy-start(bf16[2048,1024]{1,0:T(8,128)(2,1)} %get-tuple-element.48) | copy-start | bytes 12582916
  78.3 2.2 %copy-start.3 = (bf16[8,256,1024]{2,1,0:T(8,128)(2,1)S(1)}, bf16[8,256,1024]{2,1,0:T(8,128)(2,1)}, u32[]{:S(2)}) copy-start(bf16[8,256,1024]{2,1,0:T(8,128)(2,1)} %all-gather.2.cloned.1.call-done.weight_ref) | copy-start | bytes 12582916
  85.1 5.2 %collective-permute-start.7 = (bf16[4,1024,256]{2,1,0:T(8,128)(2,1)}, bf16[4,1024,256]{2,1,0:T(8,128)(2,1)}, u32[]{:S(2)}, u32[]{:S(2)}) collective-permute-start(bf16[4,1024,256]{2,1,0:T(8,128)(2,1)} %shard_map.113), channel_id=1, source_target_pairs={{0,1},{1,0},{2,3},{3,2},{4,5},{5,4},{6,7},{7,6},{8,9},{9,8},{10,11... | collective-permute-start | bytes 6291464 | tf_op jit(solution)/shard_map/ppermute | solution.py:28
  89.6 15.9 %collective-permute-start.11 = (bf16[4,1024,256]{2,1,0:T(8,128)(2,1)}, bf16[4,1024,256]{2,1,0:T(8,128)(2,1)}, u32[]{:S(2)}, u32[]{:S(2)}) collective-permute-start(bf16[4,1024,256]{2,1,0:T(8,128)(2,1)} %shard_map.116), channel_id=1, source_target_pairs={{0,1},{1,0},{2,3},{3,2},{4,5},{5,4},{6,7},{7,6},{8,9},{9,8},{10,11... | collective-permute-start | bytes 6291464 | tf_op jit(solution)/shard_map/ppermute | solution.py:28
  90.3 2.2 %copy-start.2 = (bf16[2048,1024]{1,0:T(8,128)(2,1)S(1)}, bf16[2048,1024]{1,0:T(8,128)(2,1)}, u32[]{:S(2)}) copy-start(bf16[2048,1024]{1,0:T(8,128)(2,1)} %get-tuple-element.48) | copy-start | bytes 12582916
  92.5 2.2 %copy-start.4 = (bf16[8,256,1024]{2,1,0:T(8,128)(2,1)S(1)}, bf16[8,256,1024]{2,1,0:T(8,128)(2,1)}, u32[]{:S(2)}) copy-start(bf16[8,256,1024]{2,1,0:T(8,128)(2,1)} %all-gather.2.cloned.1.call-done.weight_ref) | copy-start | bytes 12582916
  94.6 10.8 %copy-start.15 = (bf16[256]{0:T(256)(128)(2,1)S(1)}, bf16[256]{0:T(256)(128)(2,1)}, u32[]{:S(2)}) copy-start(bf16[256]{0:T(256)(128)(2,1)} %param.10) | copy-start | bytes 1540
  99.8 15.3 %collective-permute-start.8 = (bf16[1024,256]{1,0:T(8,128)(2,1)S(1)}, bf16[1024,256]{1,0:T(8,128)(2,1)S(1)}, u32[]{:S(2)}, u32[]{:S(2)}) collective-permute-start(bf16[1024,256]{1,0:T(8,128)(2,1)S(1)} %get-tuple-element.36), channel_id=1, source_target_pairs={{0,2},{2,4},{4,6},{6,0},{1,3},{3,5},{5,7},{7,1},{8,10},{10,12},{12... | collective-permute-start | bytes 1572872 | tf_op jit(solution)/shard_map/ppermute | solution.py:28
  101.4 25.7 %collective-permute-start.9 = (bf16[1024,256]{1,0:T(8,128)(2,1)S(1)}, bf16[1024,256]{1,0:T(8,128)(2,1)S(1)}, u32[]{:S(2)}, u32[]{:S(2)}) collective-permute-start(bf16[1024,256]{1,0:T(8,128)(2,1)S(1)} %get-tuple-element.37), channel_id=1, source_target_pairs={{0,4},{2,6},{4,0},{6,2},{1,5},{3,7},{5,1},{7,3},{8,12},{10,14},{12... | collective-permute-start | bytes 1572872 | tf_op jit(solution)/shard_map/ppermute | solution.py:28
  104.1 23.0 %collective-permute-start.10 = (bf16[1024,256]{1,0:T(8,128)(2,1)S(1)}, bf16[1024,256]{1,0:T(8,128)(2,1)S(1)}, u32[]{:S(2)}, u32[]{:S(2)}) collective-permute-start(bf16[1024,256]{1,0:T(8,128)(2,1)S(1)} %get-tuple-element.38), channel_id=1, source_target_pairs={{0,6},{2,0},{4,2},{6,4},{1,7},{3,1},{5,3},{7,5},{8,14},{10,8},{12,... | collective-permute-start | bytes 1572872 | tf_op jit(solution)/shard_map/ppermute | solution.py:28
  105.5 21.6 %copy-start.7 = (s32[16]{0:T(128)S(1)}, s32[16]{0:T(128)}, u32[]{:S(2)}) copy-start(s32[16]{0:T(128)} %fill_ref.3) | copy-start | bytes 196
  110.7 0.8 copy-start.8
  111.5 0.8 copy-start.9
  112.3 0.8 copy-start.10
  130.1 1.0 copy-start.5
  132.7 39.5 %all-to-all-start = ((bf16[32,64,256]{2,1,0:T(8,128)(2,1)}), bf16[32,64,256]{2,1,0:T(8,128)(2,1)}, u32[]{:S(2)}, u32[]{:S(2)}) async-start(bf16[32,64,256]{2,1,0:T(8,128)(2,1)} %copy-done.5), calls=%async_computation.2 | async-start | bytes 2097152 | tf_op jit(solution)/shard_map/all_to_all | solution.py:251
  141.6 14.5 %collective-permute-start.12 = (bf16[1024,256]{1,0:T(8,128)(2,1)}, bf16[1024,256]{1,0:T(8,128)(2,1)S(1)}, u32[]{:S(2)}, u32[]{:S(2)}) collective-permute-start(bf16[1024,256]{1,0:T(8,128)(2,1)} %copy-done.10), channel_id=1, source_target_pairs={{0,2},{2,4},{4,6},{6,0},{1,3},{3,5},{5,7},{7,1},{8,10},{10,12},{12... | collective-permute-start | bytes 1572872 | tf_op jit(solution)/shard_map/ppermute | solution.py:28
  143.0 25.2 %collective-permute-start.13 = (bf16[1024,256]{1,0:T(8,128)(2,1)}, bf16[1024,256]{1,0:T(8,128)(2,1)S(1)}, u32[]{:S(2)}, u32[]{:S(2)}) collective-permute-start(bf16[1024,256]{1,0:T(8,128)(2,1)} %copy-done.9), channel_id=1, source_target_pairs={{0,4},{2,6},{4,0},{6,2},{1,5},{3,7},{5,1},{7,3},{8,12},{10,14},{12... | collective-permute-start | bytes 1572872 | tf_op jit(solution)/shard_map/ppermute | solution.py:28
  145.4 22.8 %collective-permute-start.14 = (bf16[1024,256]{1,0:T(8,128)(2,1)}, bf16[1024,256]{1,0:T(8,128)(2,1)S(1)}, u32[]{:S(2)}, u32[]{:S(2)}) collective-permute-start(bf16[1024,256]{1,0:T(8,128)(2,1)} %copy-done.8), channel_id=1, source_target_pairs={{0,6},{2,0},{4,2},{6,4},{1,7},{3,1},{5,3},{7,5},{8,14},{10,8},{12,... | collective-permute-start | bytes 1572872 | tf_op jit(solution)/shard_map/ppermute | solution.py:28
  171.2 1.0 copy-start.6
  172.2 10.0 %copy-start.11 = (bf16[256,2048]{1,0:T(8,128)(2,1)S(1)}, bf16[256,2048]{1,0:T(8,128)(2,1)}, u32[]{:S(2)}) copy-start(bf16[256,2048]{1,0:T(8,128)(2,1)} %param.17) | copy-start | bytes 3145732
  172.2 32.2 %all-to-all-start.1 = ((bf16[32,64,256]{2,1,0:T(8,128)(2,1)}), bf16[32,64,256]{2,1,0:T(8,128)(2,1)S(1)}, u32[]{:S(2)}, u32[]{:S(2)}) async-start(bf16[32,64,256]{2,1,0:T(8,128)(2,1)} %copy-done.6), calls=%async_computation.3 | async-start | bytes 2097152 | tf_op jit(solution)/shard_map/all_to_all | solution.py:251
Sparse Core Ops, SparseCore 0:
  22.6 53.0 all-gather.1
  90.3 38.1 reduce-scatter.4
Sparse Core Ops, SparseCore 1:
  27.5 49.3 reduce-scatter.2

commit v2 on v1

v2 whole, which is shorter than its diff:
```python
import jax
import jax.numpy as jnp
from jax import lax
from jax.experimental import pallas as pl
from jax.experimental.pallas import tpu as pltpu
from jax.sharding import Mesh, PartitionSpec as P

HD = 128
PAGE = 128
EPSILON = 1e-06
ROPE_BASE = 1000000.0

Z = ("role", "zl")
ROWS = ("role", "zl", "y")
DP = ("zl", "y")
TENSOR = ("x", "core")

CHUNKS = ((0, 64), (64, 64))
ORDER = ((0, False), (1, False), (0, True), (1, True))
F32 = jnp.float32
BF16 = jnp.bfloat16


def ring(size, step):
    return [(i, (i + step) % size) for i in range(size)]


def shift(value, axis, size, step):
    return lax.ppermute(value, axis, ring(size, step))


def after(value, *earlier):
    return lax.optimization_barrier((value, earlier))[0]


def by_index(blocks, index):
    size = len(blocks)
    twice = jnp.stack(blocks + blocks[:-1])
    return lax.dynamic_slice_in_dim(twice, (size - index) % size, size, 0)


def unwritten(shape, dtype):
    return pl.pallas_call(
        lambda out_ref: None,
        out_specs=pl.BlockSpec(memory_space=pl.ANY),
        out_shape=jax.ShapeDtypeStruct(shape, dtype),
    )()


def gather_weight(weight):
    ny, y = lax.axis_size("y"), lax.axis_index("y")
    line = by_index([weight] + [shift(weight, "y", ny, -s) for s in range(1, ny)], y)
    line = line.reshape(-1, weight.shape[1])
    return lax.all_gather(line, Z, axis=0, tiled=False), line


VMEM = pl.BlockSpec(memory_space=pltpu.VMEM)
FINISH_FLOPS = 40 * 10**9
SMEM = pl.BlockSpec(memory_space=pltpu.SMEM)


def project(scaled, weight, place, other=None):
    pages, part, depth = scaled.shape
    heads, cols, _ = weight.shape
    heads //= 2
    rows = pages * part

    def kernel(place_ref, scaled_ref, weight_ref, *refs):
        rows_in = scaled_ref[...].reshape(rows, depth)
        for h in range(heads):
            head = lax.rem(place_ref[0] + h, heads)
            total = lax.dot_general(
                rows_in, weight_ref[2 * head + place_ref[1]], (((1,), (1,)), ((), ())),
                preferred_element_type=F32,
            )
            if other is None:
                refs[0][head] = total.astype(BF16)
            else:
                refs[1 + h][...] = (total + refs[0][head].astype(F32)).astype(BF16)

    if other is None:
        out_specs, out_shape = VMEM, jax.ShapeDtypeStruct((heads, rows, cols), BF16)
    else:
        out_specs = [VMEM] * heads
        out_shape = [jax.ShapeDtypeStruct((rows, cols), BF16)] * heads
    args = [place, scaled, weight] + ([] if other is None else [other])
    return pl.pallas_call(
        kernel,
        in_specs=[SMEM] + [VMEM] * (len(args) - 1),
        out_specs=out_specs,
        out_shape=out_shape,
        compiler_params=pltpu.CompilerParams(vmem_limit_bytes=24 * 2**20),
        cost_estimate=pl.CostEstimate(
            flops=2 * rows * depth * cols * heads,
            bytes_accessed=2 * (rows * depth + heads * cols * (depth + rows)),
            transcendentals=0,
        ),
    )(*args)


def finish(parts, inverse, turn, bias, target, fill, start, slots):
    pages, part, cols = parts[0].shape
    half = HD // 2

    def kernel(target_ref, fill_ref, inverse_ref, turn_ref, bias_ref, *refs):
        part_refs, out_ref = refs[:-1], refs[-1]
        out_ref[...] = jnp.zeros_like(out_ref)
        bias_row = bias_ref[...].astype(F32)
        offset = lax.broadcasted_iota(jnp.int32, (part, HD), 0) + start
        low = lax.broadcasted_iota(jnp.int32, (part, HD), 1) < half

        @pl.loop(0, pages)
        def _(page):
            total = part_refs[0][page].astype(F32)
            for part_ref in part_refs[1:]:
                total = total + part_ref[page].astype(F32)
            scale, turn = inverse_ref[page], turn_ref[page]
            swapped = pltpu.roll(turn, half, 1)
            key = total[:, :HD] * scale + bias_row[:, :HD]
            value = total[:, HD:] * scale + bias_row[:, HD:]
            key = key * jnp.where(low, turn, swapped) + pltpu.roll(key, half, 1) * jnp.where(
                low, -swapped, turn
            )
            live = offset < fill_ref[page]
            where = target_ref[page]
            out_ref[where, :, :HD] = jnp.where(live, key, 0.0).astype(BF16)
            out_ref[where, :, HD:] = jnp.where(live, value, 0.0).astype(BF16)

    return pl.pallas_call(
        kernel,
        in_specs=[SMEM, SMEM] + [VMEM] * (3 + len(parts)),
        out_specs=VMEM,
        out_shape=jax.ShapeDtypeStruct((slots, part, cols), BF16),
        compiler_params=pltpu.CompilerParams(vmem_limit_bytes=24 * 2**20),
        cost_estimate=pl.CostEstimate(
            flops=FINISH_FLOPS,
            bytes_accessed=2 * part * cols * (len(parts) * pages + slots) + 8 * pages * part * HD,
            transcendentals=0,
        ),
    )(target, fill, inverse, turn, bias, *parts)


def shards(
    kv_weight,
    kv_bias,
    norm_gain,
    page_states,
    page_replica,
    page_pos,
    page_fill,
    learn_normed,
    learn_cot,
):
    nz, ny, nx = lax.axis_size(Z), lax.axis_size("y"), lax.axis_size("x")
    core, x, y, z = (lax.axis_index(name) for name in ("core", "x", "y", Z))
    pages = page_fill.shape[0]
    depth = page_states.shape[1]
    feature_count = depth * lax.axis_size(TENSOR)
    rows = kv_weight.shape[0]

    tokens = learn_cot.shape[0]
    half = HD // 2
    replicas = lax.axis_size(DP)
    capacity = max(2, 2 * pages // replicas)
    slots = replicas * capacity

    weight, line = gather_weight(kv_weight)

    cot = after(learn_cot, line).reshape(tokens, nz, ny, rows).transpose(0, 2, 1, 3)
    terms = lax.dot_general(
        cot.reshape(tokens, -1), learn_normed, (((0,), (0,)), ((), ())), preferred_element_type=F32
    ).astype(BF16)
    terms = lax.psum_scatter(terms, "y", scatter_dimension=0, tiled=True)

    states, gain, place, owners = after(
        (page_states, norm_gain, page_pos, page_replica[:, 0]), line
    )
    widened = states.astype(F32)
    scaled = (widened * gain.astype(F32)[None, :]).astype(BF16).reshape(pages, PAGE, depth)
    squares = jnp.sum(widened * widened, axis=1).reshape(pages, PAGE)
    squares = squares + shift(squares, "core", 2, 1)
    squares = squares + shift(squares, "x", nx, 1) + shift(squares, "x", nx, 2) + shift(squares, "x", nx, 3)
    inverse = lax.rsqrt(squares / feature_count + EPSILON)
    inverse = jnp.broadcast_to(inverse[:, :, None], (pages, PAGE, HD))

    exponent = jnp.arange(half, dtype=F32) * (2.0 / HD)
    frequency = jnp.power(F32(ROPE_BASE), -exponent)
    positions = place[:, None] * PAGE + jnp.arange(PAGE, dtype=jnp.int32)[None, :]
    angles = positions.astype(F32)[:, :, None] * frequency[None, None, :]
    turn = jnp.concatenate([jnp.cos(angles), jnp.sin(angles)], axis=2)

    def in_chunks(value):
        return [value[:, start : start + part] for start, part in CHUNKS]

    scaled, inverse, turn = in_chunks(scaled), in_chunks(inverse), in_chunks(turn)

    earlier = jnp.arange(pages)[None, :] < jnp.arange(pages)[:, None]
    same = owners[:, None] == owners[None, :]
    rank = jnp.sum(jnp.where(same & earlier, 1, 0), axis=1).astype(jnp.int32)
    target = owners * capacity + rank

    weight, scaled, inverse, turn, target = lax.optimization_barrier(
        (weight, scaled, inverse, turn, target)
    )
    weight_grad = lax.psum_scatter(terms, Z, scatter_dimension=0, tiled=True)

    own, far = jnp.stack([x, core]), jnp.stack([x, 1 - core])
    away, mine, last = {}, {}, None
    for c, adds in ORDER:
        rows_in = scaled[c] if last is None else after(scaled[c], last)
        if adds:
            last = mine[c] = project(rows_in, weight, own, away[c])
        else:
            last = project(rows_in, weight, far)
            away[c] = shift(last, "core", 2, 1)

    kv_cache = unwritten((slots, PAGE, 2 * HD), BF16)
    for c, chunk in enumerate(CHUNKS):
        start, part = chunk
        parts = [m if s == 0 else shift(m, "x", nx, s) for s, m in enumerate(mine[c])]
        parts = [p.reshape(pages, part, 2 * HD) for p in parts]
        placed = finish(
            parts, inverse[c], turn[c], kv_bias[None, :], target, page_fill, start, slots
        )
        if c == 0:
            placed = after(placed, mine[len(CHUNKS) - 1])
        else:
            placed = after(placed, piece)
        if c == len(CHUNKS) - 1:
            placed = after(placed, weight_grad)
        piece = lax.all_to_all(placed, DP, 0, 0, tiled=True)
        kv_cache = lax.dynamic_update_slice(kv_cache, piece, (0, start, 0))

    learn_cot, _ = lax.optimization_barrier((learn_cot, placed))
    normed_grad = jnp.dot(
        learn_cot, weight.reshape(-1, depth), preferred_element_type=F32
    ).astype(BF16)
    return (kv_cache, normed_grad, weight_grad.astype(F32))


def solution(mesh):
    ny = 4
    nz = mesh.shape["dp"] // ny
    nx = mesh.shape["tensor"] // 2
    torus = Mesh(
        mesh.devices.reshape(mesh.shape["role"], nz, ny, nx, 2), ("role", "zl", "y", "x", "core")
    )
    placed = (
        P(ROWS, TENSOR),
        P(TENSOR),
        P(TENSOR),
        P(ROWS, TENSOR),
        P(ROWS, None),
        P(ROWS),
        P(ROWS),
        P(ROWS, TENSOR),
        P(ROWS, None),
    )
    return jax.shard_map(
        shards,
        mesh=torus,
        in_specs=placed,
        out_specs=(P(ROWS, None, TENSOR), P(ROWS, TENSOR), P(ROWS, TENSOR)),
        check_vma=False,
    )
```

time: 215 us -> 200 us (0.930)
  waiting for transfers between devices: 91.1 us -> 87.2 us
  starting transfers between devices: 38.6 us -> 35 us
  other arithmetic: 12.9 us -> 9.71 us
  local copies, waits for them, and re-layouts: 21.7 us -> 19.1 us
  Pallas kernels: 25.6 us -> 23.3 us
    ppermute x15, waiting for transfers between devices: 42.8 us -> 27.9 us  [shift(): return lax.ppermute(value, axis, ring(size, step))]
    all_to_all x2, waiting for transfers between devices: 18 us -> 29.1 us  [shards(): piece = lax.all_to_all(placed, DP, 0, 0, tiled=True)]
    unnamed x38 -> x42, local copies, waits for them, and re-layouts: 15.6 us -> 10.3 us
    neg x1 -> x0, other arithmetic: 3.72 us -> none  [shards(): sine = jnp.concatenate([-sine, sine], axis=2)]
    sin x0 -> x1, other arithmetic: none -> 3.69 us  [shards(): turn = jnp.concatenate([jnp.cos(angles), jnp.sin(angles)], axis=2)]
    pallas_call x6, Pallas kernels: 25.6 us -> 23.3 us  [the longest x4 16.1 us: project(): pl.pallas_call(kernel, in_specs=[SMEM] + [VMEM] * (len(args) - 1), out_sp...]
    all_to_all x2, starting transfers between devices: 16.5 us -> 14.2 us  [shards(): piece = lax.all_to_all(placed, DP, 0, 0, tiled=True)]
  transfers between devices with their start and end apart: 20 -> 20, of which waited for: 10 -> 10; matrix products, arithmetic and copies ran while one was open for 11% -> 13% of each run, Pallas kernels for 12% -> 12%
where the time goes in v2:
time: 200 us; the launch traced here: 197 us
  waiting for transfers between devices  87.2 us (44%)
  starting transfers between devices  35 us (18%)
  Pallas kernels  23.3 us (12%)
  local copies, waits for them, and re-layouts  19.1 us (10%)
  between operations  15.7 us (8%)
  other arithmetic  9.71 us (5%)
  matrix products  7.53 us (4%)
    all_gather x1, waiting for transfers between devices, gather_weight(): return (lax.all_gather(line, Z, axis=0, tiled=False), line)  30.1 us
    all_to_all x2, waiting for transfers between devices, shards(): piece = lax.all_to_all(placed, DP, 0, 0, tiled=True)  29.1 us
    ppermute x15, waiting for transfers between devices, shift(): return lax.ppermute(value, axis, ring(size, step))  27.9 us
    ppermute x15, starting transfers between devices, shift(): return lax.ppermute(value, axis, ring(size, step))  20.6 us
    pallas_call x4, Pallas kernels, project(): pl.pallas_call(kernel, in_specs=[SMEM] + [VMEM] * (len(args) - 1), out_sp...  16.1 us
    all_to_all x2, starting transfers between devices, shards(): piece = lax.all_to_all(placed, DP, 0, 0, tiled=True)  14.2 us
    unnamed x42, local copies, waits for them, and re-layouts  10.3 us
    pallas_call x2, Pallas kernels, finish(): pl.pallas_call(kernel, in_specs=[SMEM, SMEM] + [VMEM] * (3 + len(parts)),...  7.11 us
  transfers between devices with their start and end apart: 20, of which 10 were waited for; matrix products, arithmetic and copies ran while one was open for 13% of the time, Pallas kernels for 12%

profile of v2, /device:TPU:32, one launch (start us, length us, event | category | flops | bytes accessed | tf_op | source)
XLA Modules:
  0.0 197.5 jit_solution(17040283943950566019)
XLA Ops:
  8.1 3.1 %collective-permute-start = (bf16[64,1024]{1,0:T(8,128)(2,1)}, bf16[64,1024]{1,0:T(8,128)(2,1)S(1)}, u32[]{:S(2)}, u32[]{:S(2)}) collective-permute-start(bf16[64,1024]{1,0:T(8,128)(2,1)} %param.9), channel_id=1, source_target_pairs={{0,24},{8,0},{16,8},{24,16},{1,25},{9,1},{17,9},{25,17},{2,26},{10... | collective-permute-start | bytes 393224 | tf_op jit(solution)/shard_map/ppermute | solution.py:29
  11.1 0.6 collective-permute-start.1
  11.8 1.0 collective-permute-start.2
  12.8 0.9 bitcast_dynamic-update-slice_fusion.5
  13.7 3.3 %collective-permute-done = bf16[64,1024]{1,0:T(8,128)(2,1)S(1)} collective-permute-done((bf16[64,1024]{1,0:T(8,128)(2,1)}, bf16[64,1024]{1,0:T(8,128)(2,1)S(1)}, u32[]{:S(2)}, u32[]{:S(2)}) %collective-permute-start) | collective-permute-done | bytes 131104 | tf_op jit(solution)/shard_map/ppermute | solution.py:29
  17.0 2.2 %collective-permute-done.1 = bf16[64,1024]{1,0:T(8,128)(2,1)S(1)} collective-permute-done((bf16[64,1024]{1,0:T(8,128)(2,1)}, bf16[64,1024]{1,0:T(8,128)(2,1)S(1)}, u32[]{:S(2)}, u32[]{:S(2)}) %collective-permute-start.1) | collective-permute-done | bytes 131104 | tf_op jit(solution)/shard_map/ppermute | solution.py:29
  19.2 1.4 collective-permute-done.2
  20.6 0.9 bitcast_dynamic-update-slice_fusion.6
  21.6 0.8 constant_dynamic-slice_fusion
  22.5 1.5 copy.16
  24.1 3.3 %convolution_convert_fusion = bf16[2048,1024]{1,0:T(8,128)(2,1)} fusion(bf16[256,2048]{0,1:T(8,128)(2,1)S(1)} %bitcast.46, bf16[256,1024]{1,0:T(8,128)(2,1)S(1)} %copy-done), kind=kOutput, calls=%fused_computation.4 | convolution fusion | flops 1075838976 | bytes 5767168 | tf_op jit(solution)/shard_map/dot_general | solution.py:170
  28.1 3.5 %fusion.1 = (f32[2048]{0:T(1024)S(1)}, bf16[2048,1024]{1,0:T(8,128)(2,1)S(1)}) fusion(bf16[2048,1024]{1,0:T(8,128)(2,1)} %param.12, f32[1024]{0:T(1024)S(1)} %convert_element_type.26), kind=kLoop, calls=%fused_computation.3 | loop fusion | flops 10483712 | bytes 8400896 | tf_op jit(solution)/shard_map/reduce_sum | solution.py:180
  32.0 3.7 %multiply_sine_fusion = (f32[16,128,64]{2,1,0:T(8,128)S(1)}, f32[16,128,64]{2,1,0:T(8,128)S(1)}) fusion(f32[64]{0:T(128)S(1)} %negate_power_fusion, f32[16,128]{1,0:T(8,128)S(1)} %add_convert_fusion), kind=kLoop, calls=%fused_computation.5 | loop fusion | flops 131072 | bytes 1057024 | tf_op jit(solution)/shard_map/sin | solution.py:190
  35.7 1.8 fusion.4
  37.5 1.6 collective-permute-start.4
  39.1 2.7 %collective-permute-start.5 = (f32[16,128]{1,0:T(8,128)S(1)}, f32[16,128]{1,0:T(8,128)S(1)}, u32[]{:S(2)}, u32[]{:S(2)}) collective-permute-start(f32[16,128]{1,0:T(8,128)S(1)} %bitcast_add_fusion), channel_id=1, source_target_pairs={{0,4},{2,6},{4,0},{6,2},{1,5},{3,7},{5,1},{7,3},{8,12},{10,14},{12... | collective-permute-start | bytes 24584 | tf_op jit(solution)/shard_map/ppermute | solution.py:29
  41.8 1.4 collective-permute-start.6
  43.2 1.4 pad_maximum_fusion
  44.6 0.8 collective-permute-done.6
  45.5 30.1 %all-gather.2.cloned.1.call-done.weight_ref = bf16[8,256,1024]{2,1,0:T(8,128)(2,1)} async-done(((bf16[1,256,1024]{2,1,0:T(8,128)(2,1)}), bf16[8,256,1024]{2,1,0:T(8,128)(2,1)}) %all-gather.2.cloned.1.call-update) | async-done | bytes 4194320 | tf_op jit(solution)/shard_map/all_gather | solution.py:54
  75.7 1.0 broadcast_in_dim.12.inverse_ref
  76.9 2.2 %copy-done.1 = bf16[8,256,1024]{2,1,0:T(8,128)(2,1)S(1)} copy-done((bf16[8,256,1024]{2,1,0:T(8,128)(2,1)S(1)}, bf16[8,256,1024]{2,1,0:T(8,128)(2,1)}, u32[]{:S(2)}) %copy-start.1) | copy-done | bytes 4194328
  79.1 1.6 copy-done.3
  80.7 2.9 %shard_map.113 = bf16[4,1024,256]{2,1,0:T(8,128)(2,1)S(1)} custom-call(s32[2]{0:T(128)S(1)} %pad_add_fusion.1.place_ref, bf16[16,64,1024]{2,1,0:T(8,128)(2,1)S(1)} %copy-done.3, bf16[8,256,1024]{2,1,0:T(8,128)(2,1)S(1)} %copy-done.1), custom_call_target="tpu_custom_call" | custom-call | flops 2147483648 | bytes 6291456 | tf_op jit(solution)/shard_map/pallas_call | solution.py:87
  83.7 4.2 %shard_map.114 = bf16[4,1024,256]{2,1,0:T(8,128)(2,1)} custom-call(s32[2]{0:T(128)S(1)} %pad_add_fusion.1.place_ref, bf16[16,64,1024]{2,1,0:T(8,128)(2,1)S(1)} %get-tuple-element.47.scaled_ref, bf16[8,256,1024]{2,1,0:T(8,128)(2,1)S(1)} %copy-done.1), custom_call_target="tpu_custom_call" | custom-call | flops 2147483648 | bytes 6291456 | tf_op jit(solution)/shard_map/pallas_call | solution.py:87
  88.5 3.9 %shard_map.115 = (bf16[1024,256]{1,0:T(8,128)(2,1)S(1)}, bf16[1024,256]{1,0:T(8,128)(2,1)}, bf16[1024,256]{1,0:T(8,128)(2,1)}, bf16[1024,256]{1,0:T(8,128)(2,1)}) custom-call(s32[2]{0:T(128)S(1)} %pad_add_fusion.place_ref, bf16[16,64,1024]{2,1,0:T(8,128)(2,1)S(1)} %copy-done.3, bf16[8,256,1024]{2,1,0:T(8,128)(2,1)S(1)} %copy-done.1, ...), custom_call_target="tpu_custom_call" | custom-call | flops 2147483648 | bytes 6291456 | tf_op jit(solution)/shard_map/pallas_call | solution.py:87
  92.4 0.8 copy-done.7
  93.2 1.5 collective-permute-start.8
  94.7 2.7 %collective-permute-start.9 = (bf16[1024,256]{1,0:T(8,128)(2,1)}, bf16[1024,256]{1,0:T(8,128)(2,1)}, u32[]{:S(2)}, u32[]{:S(2)}) collective-permute-start(bf16[1024,256]{1,0:T(8,128)(2,1)} %get-tuple-element.45), channel_id=1, source_target_pairs={{0,4},{2,6},{4,0},{6,2},{1,5},{3,7},{5,1},{7,3},{8,12},{10,14},{12... | collective-permute-start | bytes 1572872 | tf_op jit(solution)/shard_map/ppermute | solution.py:29
  97.4 1.5 collective-permute-start.10
  98.9 2.2 %copy-done.2 = bf16[8,256,1024]{2,1,0:T(8,128)(2,1)S(1)} copy-done((bf16[8,256,1024]{2,1,0:T(8,128)(2,1)S(1)}, bf16[8,256,1024]{2,1,0:T(8,128)(2,1)}, u32[]{:S(2)}) %copy-start.2) | copy-done | bytes 4194328
  101.1 5.1 %shard_map.117 = (bf16[1024,256]{1,0:T(8,128)(2,1)S(1)}, bf16[1024,256]{1,0:T(8,128)(2,1)}, bf16[1024,256]{1,0:T(8,128)(2,1)}, bf16[1024,256]{1,0:T(8,128)(2,1)}) custom-call(s32[2]{0:T(128)S(1)} %pad_add_fusion.place_ref, bf16[16,64,1024]{2,1,0:T(8,128)(2,1)S(1)} %get-tuple-element.47.scaled_ref, bf16[8,256,1024]{2,1,0:T(8,128)(2,1)S(1)} %copy-done.2, ...), custom_call_target="tpu_custom_call" | custom-call | flops 2147483648 | bytes 6291456 | tf_op jit(solution)/shard_map/pallas_call | solution.py:87
  106.7 0.9 collective-permute-start.13
  107.7 0.9 collective-permute-done.8
  108.6 2.4 %collective-permute-start.14 = (bf16[1024,256]{1,0:T(8,128)(2,1)}, bf16[1024,256]{1,0:T(8,128)(2,1)S(1)}, u32[]{:S(2)}, u32[]{:S(2)}) collective-permute-start(bf16[1024,256]{1,0:T(8,128)(2,1)} %get-tuple-element.51), channel_id=1, source_target_pairs={{0,6},{2,0},{4,2},{6,4},{1,7},{3,1},{5,3},{7,5},{8,14},{10,8},{12,... | collective-permute-start | bytes 1572872 | tf_op jit(solution)/shard_map/ppermute | solution.py:29
  111.0 10.7 %collective-permute-done.9 = bf16[1024,256]{1,0:T(8,128)(2,1)} collective-permute-done((bf16[1024,256]{1,0:T(8,128)(2,1)}, bf16[1024,256]{1,0:T(8,128)(2,1)}, u32[]{:S(2)}, u32[]{:S(2)}) %collective-permute-start.9) | collective-permute-done | bytes 524320 | tf_op jit(solution)/shard_map/ppermute | solution.py:29
  121.8 4.0 %shard_map.116 = bf16[32,64,256]{2,1,0:T(8,128)(2,1)} custom-call(s32[16]{0:T(128)S(1)} %multiply_add_fusion.target_ref, s32[16]{0:T(128)S(1)} %copy-done.11, f32[16,64,128]{2,1,0:T(8,128)S(1)} %copy-done.4, f32[16,64,128]{2,1,0:T(8,128)S(1)} %copy-done.6, bf16[1,256]{1,0:T(2,128)(2,1)S(1)} %broadcast_in_dim.18.bias_ref, bf16[16,64,256]{2,1,0:T(8,128)(2,1)S(1)} %bitcast.40, ...), custom_call_target="tpu_custom_call" | custom-call | flops 40000000000 | bytes 4194304 | tf_op jit(solution)/shard_map/pallas_call | solution.py:129
  125.7 9.0 %all-to-all-start = ((bf16[32,64,256]{2,1,0:T(8,128)(2,1)}), bf16[32,64,256]{2,1,0:T(8,128)(2,1)}, u32[]{:S(2)}, u32[]{:S(2)}) async-start(bf16[32,64,256]{2,1,0:T(8,128)(2,1)} %shard_map.116), calls=%async_computation | async-start | bytes 2097152 | tf_op jit(solution)/shard_map/all_to_all | solution.py:231
  134.7 8.4 %collective-permute-done.13 = bf16[1024,256]{1,0:T(8,128)(2,1)S(1)} collective-permute-done((bf16[1024,256]{1,0:T(8,128)(2,1)}, bf16[1024,256]{1,0:T(8,128)(2,1)S(1)}, u32[]{:S(2)}, u32[]{:S(2)}) %collective-permute-start.13) | collective-permute-done | bytes 524320 | tf_op jit(solution)/shard_map/ppermute | solution.py:29
  143.2 1.0 copy-done.10
  144.2 3.1 %shard_map.118 = bf16[32,64,256]{2,1,0:T(8,128)(2,1)} custom-call(s32[16]{0:T(128)S(1)} %multiply_add_fusion.target_ref, s32[16]{0:T(128)S(1)} %copy-done.11, f32[16,64,128]{2,1,0:T(8,128)S(1)} %broadcast_in_dim.13.inverse_ref, f32[16,64,128]{2,1,0:T(8,128)S(1)} %copy-done.5, bf16[1,256]{1,0:T(2,128)(2,1)S(1)} %broadcast_in_dim.18.bias_ref, ...), custom_call_target="tpu_custom_call" | custom-call | flops 40000000000 | bytes 4194304 | tf_op jit(solution)/shard_map/pallas_call | solution.py:129
  147.3 11.6 %all-to-all-done = bf16[32,64,256]{2,1,0:T(8,128)(2,1)} async-done(((bf16[32,64,256]{2,1,0:T(8,128)(2,1)}), bf16[32,64,256]{2,1,0:T(8,128)(2,1)}, u32[]{:S(2)}, u32[]{:S(2)}) %all-to-all-start) | async-done | bytes 1048608 | tf_op jit(solution)/shard_map/all_to_all | solution.py:231
  159.0 5.3 %all-to-all-start.1 = ((bf16[32,64,256]{2,1,0:T(8,128)(2,1)}), bf16[32,64,256]{2,1,0:T(8,128)(2,1)S(1)}, u32[]{:S(2)}, u32[]{:S(2)}) async-start(bf16[32,64,256]{2,1,0:T(8,128)(2,1)} %shard_map.118), calls=%async_computation.3 | async-start | bytes 2097152 | tf_op jit(solution)/shard_map/all_to_all | solution.py:231
  164.3 0.7 convert_element_type.31
  165.0 2.3 %constant_dynamic-update-slice_fusion.1 = bf16[32,128,256]{2,1,0:T(8,128)(2,1)} fusion(bf16[32,128,256]{2,1,0:T(8,128)(2,1)} %shard_map.112, bf16[32,64,256]{2,1,0:T(8,128)(2,1)} %all-to-all-done), kind=kLoop, calls=%fused_computation.25 | loop fusion | bytes 2097152 | tf_op jit(solution)/shard_map/dynamic_update_slice | solution.py:232
  167.3 4.2 %convolution_convert_fusion.1 = bf16[256,1024]{1,0:T(8,128)(2,1)} fusion(bf16[256,2048]{1,0:T(8,128)(2,1)S(1)} %copy-done.12, bf16[2048,1024]{1,0:T(8,128)(2,1)} %bitcast.39), kind=kOutput, calls=%fused_computation.7 | convolution fusion | flops 1074003968 | bytes 5767168 | tf_op jit(solution)/shard_map/dot_general | solution.py:235
  171.5 17.5 %all-to-all-done.1 = bf16[32,64,256]{2,1,0:T(8,128)(2,1)S(1)} async-done(((bf16[32,64,256]{2,1,0:T(8,128)(2,1)}), bf16[32,64,256]{2,1,0:T(8,128)(2,1)S(1)}, u32[]{:S(2)}, u32[]{:S(2)}) %all-to-all-start.1) | async-done | bytes 1048608 | tf_op jit(solution)/shard_map/all_to_all | solution.py:231
  189.0 1.0 constant_dynamic-update-slice_fusion
  (71 shorter events, 2.8 us)
Async XLA Ops:
  8.0 16.1 %copy-start = (bf16[256,1024]{1,0:T(8,128)(2,1)S(1)}, bf16[256,1024]{1,0:T(8,128)(2,1)}, u32[]{:S(2)}) copy-start(bf16[256,1024]{1,0:T(8,128)(2,1)} %param.16) | copy-start | bytes 1572868
  8.0 67.7 %all-gather.2.cloned.1.call-start = ((), (), s32[]{:S(2)}) async-start(), calls=%async_computation.4 | async-start | bytes 4718592 | tf_op jit(solution)/shard_map/all_gather | solution.py:54
  8.1 9.0 %collective-permute-start = (bf16[64,1024]{1,0:T(8,128)(2,1)}, bf16[64,1024]{1,0:T(8,128)(2,1)S(1)}, u32[]{:S(2)}, u32[]{:S(2)}) collective-permute-start(bf16[64,1024]{1,0:T(8,128)(2,1)} %param.9), channel_id=1, source_target_pairs={{0,24},{8,0},{16,8},{24,16},{1,25},{9,1},{17,9},{25,17},{2,26},{10... | collective-permute-start | bytes 393224 | tf_op jit(solution)/shard_map/ppermute | solution.py:29
  11.1 8.1 %collective-permute-start.1 = (bf16[64,1024]{1,0:T(8,128)(2,1)}, bf16[64,1024]{1,0:T(8,128)(2,1)S(1)}, u32[]{:S(2)}, u32[]{:S(2)}) collective-permute-start(bf16[64,1024]{1,0:T(8,128)(2,1)} %param.9), channel_id=1, source_target_pairs={{0,16},{8,24},{16,0},{24,8},{1,17},{9,25},{17,1},{25,9},{2,18},{10... | collective-permute-start | bytes 393224 | tf_op jit(solution)/shard_map/ppermute | solution.py:29
  11.8 8.8 %collective-permute-start.2 = (bf16[64,1024]{1,0:T(8,128)(2,1)}, bf16[64,1024]{1,0:T(8,128)(2,1)S(1)}, u32[]{:S(2)}, u32[]{:S(2)}) collective-permute-start(bf16[64,1024]{1,0:T(8,128)(2,1)} %param.9), channel_id=1, source_target_pairs={{0,8},{8,16},{16,24},{24,0},{1,9},{9,17},{17,25},{25,1},{2,10},{10... | collective-permute-start | bytes 393224 | tf_op jit(solution)/shard_map/ppermute | solution.py:29
  22.5 76.4 %reduce-scatter.3.cloned.1.call-start = ((), (), s32[]{:S(2)}) async-start(), calls=%async_computation.5 | async-start | bytes 5242880 | tf_op jit(solution)/shard_map/reduce_scatter | solution.py:173
  27.4 0.7 copy-start.14
  27.4 131.6 %reduce-scatter.5.cloned.1.call-start = ((), (), s32[]{:S(2)}) async-start(), calls=%async_computation.6 | async-start | bytes 1179648 | tf_op jit(solution)/shard_map/reduce_scatter | solution.py:205
  28.1 3.6 %copy-start.16 = (s32[16,1]{0,1:T(1,128)S(1)}, s32[16,1]{0,1:T(1,128)}, u32[]{:S(2)}) copy-start(s32[16,1]{0,1:T(1,128)} %param.13) | copy-start | bytes 196
  28.1 3.8 %copy-start.15 = (s32[16]{0:T(128)S(1)}, s32[16]{0:T(128)}, u32[]{:S(2)}) copy-start(s32[16]{0:T(128)} %param.14) | copy-start | bytes 196
  31.6 5.9 %collective-permute-start.3 = (f32[16,128]{1,0:T(8,128)S(1)}, f32[16,128]{1,0:T(8,128)S(1)}, u32[]{:S(2)}, u32[]{:S(2)}) collective-permute-start(f32[16,128]{1,0:T(8,128)S(1)} %bitcast.49), channel_id=1, source_target_pairs={{0,1},{1,0},{2,3},{3,2},{4,5},{5,4},{6,7},{7,6},{8,9},{9,8},{10,11... | collective-permute-start | bytes 24584 | tf_op jit(solution)/shard_map/ppermute | solution.py:29
  37.5 7.1 %collective-permute-start.4 = (f32[16,128]{1,0:T(8,128)S(1)}, f32[16,128]{1,0:T(8,128)S(1)}, u32[]{:S(2)}, u32[]{:S(2)}) collective-permute-start(f32[16,128]{1,0:T(8,128)S(1)} %bitcast_add_fusion), channel_id=1, source_target_pairs={{0,2},{2,4},{4,6},{6,0},{1,3},{3,5},{5,7},{7,1},{8,10},{10,12},{12... | collective-permute-start | bytes 24584 | tf_op jit(solution)/shard_map/ppermute | solution.py:29
  39.1 5.5 %collective-permute-start.5 = (f32[16,128]{1,0:T(8,128)S(1)}, f32[16,128]{1,0:T(8,128)S(1)}, u32[]{:S(2)}, u32[]{:S(2)}) collective-permute-start(f32[16,128]{1,0:T(8,128)S(1)} %bitcast_add_fusion), channel_id=1, source_target_pairs={{0,4},{2,6},{4,0},{6,2},{1,5},{3,7},{5,1},{7,3},{8,12},{10,14},{12... | collective-permute-start | bytes 24584 | tf_op jit(solution)/shard_map/ppermute | solution.py:29
  41.8 3.7 %collective-permute-start.6 = (f32[16,128]{1,0:T(8,128)S(1)}, f32[16,128]{1,0:T(8,128)S(1)}, u32[]{:S(2)}, u32[]{:S(2)}) collective-permute-start(f32[16,128]{1,0:T(8,128)S(1)} %bitcast_add_fusion), channel_id=1, source_target_pairs={{0,6},{2,0},{4,2},{6,4},{1,7},{3,1},{5,3},{7,5},{8,14},{10,8},{12,... | collective-permute-start | bytes 24584 | tf_op jit(solution)/shard_map/ppermute | solution.py:29
  76.9 2.2 %copy-start.1 = (bf16[8,256,1024]{2,1,0:T(8,128)(2,1)S(1)}, bf16[8,256,1024]{2,1,0:T(8,128)(2,1)}, u32[]{:S(2)}) copy-start(bf16[8,256,1024]{2,1,0:T(8,128)(2,1)} %all-gather.2.cloned.1.call-done.weight_ref) | copy-start | bytes 12582916
  79.1 1.6 copy-start.3
  83.6 4.9 %collective-permute-start.7 = (bf16[4,1024,256]{2,1,0:T(8,128)(2,1)S(1)}, bf16[4,1024,256]{2,1,0:T(8,128)(2,1)S(1)}, u32[]{:S(2)}, u32[]{:S(2)}) collective-permute-start(bf16[4,1024,256]{2,1,0:T(8,128)(2,1)S(1)} %shard_map.113), channel_id=1, source_target_pairs={{0,1},{1,0},{2,3},{3,2},{4,5},{5,4},{6,7},{7,6},{8,9},{9,8},{10,11... | collective-permute-start | bytes 6291464 | tf_op jit(solution)/shard_map/ppermute | solution.py:29
  87.9 10.9 %collective-permute-start.11 = (bf16[4,1024,256]{2,1,0:T(8,128)(2,1)}, bf16[4,1024,256]{2,1,0:T(8,128)(2,1)}, u32[]{:S(2)}, u32[]{:S(2)}) collective-permute-start(bf16[4,1024,256]{2,1,0:T(8,128)(2,1)} %shard_map.114), channel_id=1, source_target_pairs={{0,1},{1,0},{2,3},{3,2},{4,5},{5,4},{6,7},{7,6},{8,9},{9,8},{10,11... | collective-permute-start | bytes 6291464 | tf_op jit(solution)/shard_map/ppermute | solution.py:29
  88.5 10.3 %copy-start.17 = (bf16[256]{0:T(256)(128)(2,1)S(1)}, bf16[256]{0:T(256)(128)(2,1)}, u32[]{:S(2)}) copy-start(bf16[256]{0:T(256)(128)(2,1)} %param.10) | copy-start | bytes 1540
  92.4 0.8 copy-start.7
  93.2 15.4 %collective-permute-start.8 = (bf16[1024,256]{1,0:T(8,128)(2,1)}, bf16[1024,256]{1,0:T(8,128)(2,1)}, u32[]{:S(2)}, u32[]{:S(2)}) collective-permute-start(bf16[1024,256]{1,0:T(8,128)(2,1)} %get-tuple-element.44), channel_id=1, source_target_pairs={{0,2},{2,4},{4,6},{6,0},{1,3},{3,5},{5,7},{7,1},{8,10},{10,12},{12... | collective-permute-start | bytes 1572872 | tf_op jit(solution)/shard_map/ppermute | solution.py:29
  94.7 27.0 %collective-permute-start.9 = (bf16[1024,256]{1,0:T(8,128)(2,1)}, bf16[1024,256]{1,0:T(8,128)(2,1)}, u32[]{:S(2)}, u32[]{:S(2)}) collective-permute-start(bf16[1024,256]{1,0:T(8,128)(2,1)} %get-tuple-element.45), channel_id=1, source_target_pairs={{0,4},{2,6},{4,0},{6,2},{1,5},{3,7},{5,1},{7,3},{8,12},{10,14},{12... | collective-permute-start | bytes 1572872 | tf_op jit(solution)/shard_map/ppermute | solution.py:29
  97.4 24.4 %collective-permute-start.10 = (bf16[1024,256]{1,0:T(8,128)(2,1)}, bf16[1024,256]{1,0:T(8,128)(2,1)}, u32[]{:S(2)}, u32[]{:S(2)}) collective-permute-start(bf16[1024,256]{1,0:T(8,128)(2,1)} %get-tuple-element.46), channel_id=1, source_target_pairs={{0,6},{2,0},{4,2},{6,4},{1,7},{3,1},{5,3},{7,5},{8,14},{10,8},{12,... | collective-permute-start | bytes 1572872 | tf_op jit(solution)/shard_map/ppermute | solution.py:29
  98.9 2.2 %copy-start.2 = (bf16[8,256,1024]{2,1,0:T(8,128)(2,1)S(1)}, bf16[8,256,1024]{2,1,0:T(8,128)(2,1)}, u32[]{:S(2)}) copy-start(bf16[8,256,1024]{2,1,0:T(8,128)(2,1)} %all-gather.2.cloned.1.call-done.weight_ref) | copy-start | bytes 12582916
  101.1 20.7 %copy-start.4 = (f32[16,64,128]{2,1,0:T(8,128)S(1)}, f32[16,64,128]{2,1,0:T(8,128)}, u32[]{:S(2)}) copy-start(f32[16,64,128]{2,1,0:T(8,128)} %broadcast_in_dim.12.inverse_ref) | copy-start | bytes 1572868
  101.1 20.7 %copy-start.6 = (f32[16,64,128]{2,1,0:T(8,128)S(1)}, f32[16,64,128]{2,1,0:T(8,128)}, u32[]{:S(2)}) copy-start(f32[16,64,128]{2,1,0:T(8,128)} %get-tuple-element.37.turn_ref) | copy-start | bytes 1572868
  101.1 20.7 %copy-start.8 = (bf16[1024,256]{1,0:T(8,128)(2,1)S(1)}, bf16[1024,256]{1,0:T(8,128)(2,1)}, u32[]{:S(2)}) copy-start(bf16[1024,256]{1,0:T(8,128)(2,1)} %copy-done.7) | copy-start | bytes 1572868
  101.1 20.7 %copy-start.11 = (s32[16]{0:T(128)S(1)}, s32[16]{0:T(128)}, u32[]{:S(2)}) copy-start(s32[16]{0:T(128)} %fill_ref.3) | copy-start | bytes 196
  106.2 19.6 %copy-start.9 = (bf16[1024,256]{1,0:T(8,128)(2,1)}, bf16[1024,256]{1,0:T(8,128)(2,1)S(1)}, u32[]{:S(2)}) copy-start(bf16[1024,256]{1,0:T(8,128)(2,1)S(1)} %get-tuple-element.48) | copy-start | bytes 1572868
  106.2 28.5 %collective-permute-start.12 = (bf16[1024,256]{1,0:T(8,128)(2,1)}, bf16[1024,256]{1,0:T(8,128)(2,1)S(1)}, u32[]{:S(2)}, u32[]{:S(2)}) collective-permute-start(bf16[1024,256]{1,0:T(8,128)(2,1)} %get-tuple-element.49), channel_id=1, source_target_pairs={{0,2},{2,4},{4,6},{6,0},{1,3},{3,5},{5,7},{7,1},{8,10},{10,12},{12... | collective-permute-start | bytes 1572872 | tf_op jit(solution)/shard_map/ppermute | solution.py:29
  106.7 36.4 %collective-permute-start.13 = (bf16[1024,256]{1,0:T(8,128)(2,1)}, bf16[1024,256]{1,0:T(8,128)(2,1)S(1)}, u32[]{:S(2)}, u32[]{:S(2)}) collective-permute-start(bf16[1024,256]{1,0:T(8,128)(2,1)} %get-tuple-element.50), channel_id=1, source_target_pairs={{0,4},{2,6},{4,0},{6,2},{1,5},{3,7},{5,1},{7,3},{8,12},{10,14},{12... | collective-permute-start | bytes 1572872 | tf_op jit(solution)/shard_map/ppermute | solution.py:29
  108.6 34.5 %collective-permute-start.14 = (bf16[1024,256]{1,0:T(8,128)(2,1)}, bf16[1024,256]{1,0:T(8,128)(2,1)S(1)}, u32[]{:S(2)}, u32[]{:S(2)}) collective-permute-start(bf16[1024,256]{1,0:T(8,128)(2,1)} %get-tuple-element.51), channel_id=1, source_target_pairs={{0,6},{2,0},{4,2},{6,4},{1,7},{3,1},{5,3},{7,5},{8,14},{10,8},{12,... | collective-permute-start | bytes 1572872 | tf_op jit(solution)/shard_map/ppermute | solution.py:29
  121.8 21.4 %copy-start.5 = (f32[16,64,128]{2,1,0:T(8,128)S(1)}, f32[16,64,128]{2,1,0:T(8,128)}, u32[]{:S(2)}) copy-start(f32[16,64,128]{2,1,0:T(8,128)} %get-tuple-element.54.turn_ref) | copy-start | bytes 1572868
  125.7 33.2 %all-to-all-start = ((bf16[32,64,256]{2,1,0:T(8,128)(2,1)}), bf16[32,64,256]{2,1,0:T(8,128)(2,1)}, u32[]{:S(2)}, u32[]{:S(2)}) async-start(bf16[32,64,256]{2,1,0:T(8,128)(2,1)} %shard_map.116), calls=%async_computation | async-start | bytes 2097152 | tf_op jit(solution)/shard_map/all_to_all | solution.py:231
  143.1 1.0 copy-start.10
  147.3 20.0 %copy-start.12 = (bf16[256,2048]{1,0:T(8,128)(2,1)S(1)}, bf16[256,2048]{1,0:T(8,128)(2,1)}, u32[]{:S(2)}) copy-start(bf16[256,2048]{1,0:T(8,128)(2,1)} %param.17) | copy-start | bytes 3145732
  159.0 5.3 %copy-start.13 = (bf16[64,1024]{1,0:T(8,128)(2,1)S(1)}, bf16[64,1024]{1,0:T(8,128)(2,1)}, u32[]{:S(2)}) copy-start(bf16[64,1024]{1,0:T(8,128)(2,1)} %reduce-scatter.5.cloned.1.call-done) | copy-start | bytes 393220
  159.0 30.0 %all-to-all-start.1 = ((bf16[32,64,256]{2,1,0:T(8,128)(2,1)}), bf16[32,64,256]{2,1,0:T(8,128)(2,1)S(1)}, u32[]{:S(2)}, u32[]{:S(2)}) async-start(bf16[32,64,256]{2,1,0:T(8,128)(2,1)} %shard_map.118), calls=%async_computation.3 | async-start | bytes 2097152 | tf_op jit(solution)/shard_map/all_to_all | solution.py:231
Sparse Core Ops, SparseCore 0:
  22.6 53.0 all-gather.1
  99.0 35.9 reduce-scatter.4
Sparse Core Ops, SparseCore 1:
  27.5 49.3 reduce-scatter.2

commit v3 on v2

--- a/solution.py
+++ b/solution.py
@@ -15,8 +15,8 @@
 DP = ("zl", "y")
 TENSOR = ("x", "core")
 
-CHUNKS = ((0, 64), (64, 64))
-ORDER = ((0, False), (1, False), (0, True), (1, True))
+CHUNKS = ((0, 48), (48, 80))
+ORDER = ((0, False), (0, True), (1, False), (1, True))
 F32 = jnp.float32
 BF16 = jnp.bfloat16
 
@@ -176,12 +176,15 @@
         (page_states, norm_gain, page_pos, page_replica[:, 0]), line
     )
     widened = states.astype(F32)
-    scaled = (widened * gain.astype(F32)[None, :]).astype(BF16).reshape(pages, PAGE, depth)
+    by_page = states.reshape(pages, PAGE, depth)
+    scaled = [
+        (by_page[:, start : start + part].astype(F32) * gain.astype(F32)[None, None, :]).astype(BF16)
+        for start, part in CHUNKS
+    ]
     squares = jnp.sum(widened * widened, axis=1).reshape(pages, PAGE)
     squares = squares + shift(squares, "core", 2, 1)
     squares = squares + shift(squares, "x", nx, 1) + shift(squares, "x", nx, 2) + shift(squares, "x", nx, 3)
     inverse = lax.rsqrt(squares / feature_count + EPSILON)
-    inverse = jnp.broadcast_to(inverse[:, :, None], (pages, PAGE, HD))
 
     exponent = jnp.arange(half, dtype=F32) * (2.0 / HD)
     frequency = jnp.power(F32(ROPE_BASE), -exponent)
@@ -192,7 +195,7 @@
     def in_chunks(value):
         return [value[:, start : start + part] for start, part in CHUNKS]
 
-    scaled, inverse, turn = in_chunks(scaled), in_chunks(inverse), in_chunks(turn)
+    turn = in_chunks(turn)
 
     earlier = jnp.arange(pages)[None, :] < jnp.arange(pages)[:, None]
     same = owners[:, None] == owners[None, :]
@@ -204,6 +207,7 @@
     )
     weight_grad = lax.psum_scatter(terms, Z, scatter_dimension=0, tiled=True)
 
+    inverse = in_chunks(jnp.broadcast_to(inverse[:, :, None], (pages, PAGE, HD)))
     own, far = jnp.stack([x, core]), jnp.stack([x, 1 - core])
     away, mine, last = {}, {}, None
     for c, adds in ORDER:
@@ -223,7 +227,7 @@
             parts, inverse[c], turn[c], kv_bias[None, :], target, page_fill, start, slots
         )
         if c == 0:
-            placed = after(placed, mine[len(CHUNKS) - 1])
+            placed = after(placed, mine[len(CHUNKS) - 1], inverse[1:])
         else:
             placed = after(placed, piece)
         if c == len(CHUNKS) - 1:

time: 200 us -> 197 us (0.985); the launches traced: 197 us -> 197 us
  local copies, waits for them, and re-layouts: 19.1 us -> 13.9 us
  other arithmetic: 9.71 us -> 12.7 us
  starting transfers between devices: 35 us -> 37.6 us
    all_to_all x2, waiting for transfers between devices: 29.1 us -> 25.2 us  [shards(): piece = lax.all_to_all(placed, DP, 0, 0, tiled=True)]
    sin x1 -> x0, other arithmetic: 3.69 us -> none  [shards(): turn = jnp.concatenate([jnp.cos(angles), jnp.sin(angles)], axis=2)]
    cos x0 -> x1, other arithmetic: none -> 3.69 us  [shards(): turn = jnp.concatenate([jnp.cos(angles), jnp.sin(angles)], axis=2)]
    ppermute x15, waiting for transfers between devices: 27.9 us -> 30.7 us  [shift(): return lax.ppermute(value, axis, ring(size, step))]
    convert_element_type x1 -> x3, other arithmetic: 0.01 us -> 2.69 us  [the longest x2 2.69 us: shards(): (by_page[:, start:start + part].astype(F32) * gain.astype(F32)[None, None...]
    all_to_all x2, starting transfers between devices: 14.2 us -> 16.8 us  [shards(): piece = lax.all_to_all(placed, DP, 0, 0, tiled=True)]
    unnamed x42 -> x50, local copies, waits for them, and re-layouts: 10.3 us -> 8.2 us
  transfers between devices with their start and end apart: 20 -> 20, of which waited for: 10 -> 12; matrix products, arithmetic and copies ran while one was open for 13% -> 13% of each run, Pallas kernels for 12% -> 12%
where the time goes in v3:
time: 197 us
  waiting for transfers between devices  85.3 us (43%)
  starting transfers between devices  37.6 us (19%)
  Pallas kernels  24 us (12%)
  between operations  15.8 us (8%)
  local copies, waits for them, and re-layouts  13.9 us (7%)
  other arithmetic  12.7 us (6%)
  matrix products  7.53 us (4%)
    ppermute x15, waiting for transfers between devices, shift(): return lax.ppermute(value, axis, ring(size, step))  30.7 us
    all_gather x1, waiting for transfers between devices, gather_weight(): return (lax.all_gather(line, Z, axis=0, tiled=False), line)  29.4 us
    all_to_all x2, waiting for transfers between devices, shards(): piece = lax.all_to_all(placed, DP, 0, 0, tiled=True)  25.2 us
    ppermute x15, starting transfers between devices, shift(): return lax.ppermute(value, axis, ring(size, step))  20.7 us
    all_to_all x2, starting transfers between devices, shards(): piece = lax.all_to_all(placed, DP, 0, 0, tiled=True)  16.8 us
    pallas_call x4, Pallas kernels, project(): pl.pallas_call(kernel, in_specs=[SMEM] + [VMEM] * (len(args) - 1), out_sp...  16.3 us
    unnamed x50, local copies, waits for them, and re-layouts  8.2 us
    pallas_call x2, Pallas kernels, finish(): pl.pallas_call(kernel, in_specs=[SMEM, SMEM] + [VMEM] * (3 + len(parts)),...  7.63 us
  transfers between devices with their start and end apart: 20, of which 12 were waited for; matrix products, arithmetic and copies ran while one was open for 13% of the time, Pallas kernels for 12%

profile of v3, /device:TPU:32, one launch (start us, length us, event | category | flops | bytes accessed | tf_op | source)
XLA Modules:
  0.0 196.8 jit_solution(5696309410667952927)
XLA Ops:
  8.1 3.1 %collective-permute-start = (bf16[64,1024]{1,0:T(8,128)(2,1)}, bf16[64,1024]{1,0:T(8,128)(2,1)S(1)}, u32[]{:S(2)}, u32[]{:S(2)}) collective-permute-start(bf16[64,1024]{1,0:T(8,128)(2,1)} %param.9), channel_id=1, source_target_pairs={{0,24},{8,0},{16,8},{24,16},{1,25},{9,1},{17,9},{25,17},{2,26},{10... | collective-permute-start | bytes 393224 | tf_op jit(solution)/shard_map/ppermute | solution.py:29
  11.2 0.6 collective-permute-start.1
  11.8 1.0 collective-permute-start.2
  12.8 0.9 bitcast_dynamic-update-slice_fusion.5
  13.7 3.3 %collective-permute-done = bf16[64,1024]{1,0:T(8,128)(2,1)S(1)} collective-permute-done((bf16[64,1024]{1,0:T(8,128)(2,1)}, bf16[64,1024]{1,0:T(8,128)(2,1)S(1)}, u32[]{:S(2)}, u32[]{:S(2)}) %collective-permute-start) | collective-permute-done | bytes 131104 | tf_op jit(solution)/shard_map/ppermute | solution.py:29
  17.1 2.2 %collective-permute-done.1 = bf16[64,1024]{1,0:T(8,128)(2,1)S(1)} collective-permute-done((bf16[64,1024]{1,0:T(8,128)(2,1)}, bf16[64,1024]{1,0:T(8,128)(2,1)S(1)}, u32[]{:S(2)}, u32[]{:S(2)}) %collective-permute-start.1) | collective-permute-done | bytes 131104 | tf_op jit(solution)/shard_map/ppermute | solution.py:29
  19.3 1.4 collective-permute-done.2
  20.7 0.9 bitcast_dynamic-update-slice_fusion.6
  21.6 0.8 constant_dynamic-slice_fusion
  23.2 3.3 %convolution_convert_fusion = bf16[2048,1024]{1,0:T(8,128)(2,1)} fusion(bf16[256,2048]{0,1:T(8,128)(2,1)S(1)} %bitcast.47, bf16[256,1024]{1,0:T(8,128)(2,1)S(1)} %copy-done), kind=kOutput, calls=%fused_computation.2 | convolution fusion | flops 1075838976 | bytes 5767168 | tf_op jit(solution)/shard_map/dot_general | solution.py:170
  26.7 3.2 %multiply_reduce_fusion = f32[2048]{0:T(1024)S(1)} fusion(bf16[2048,1024]{1,0:T(8,128)(2,1)} %param.12), kind=kLoop, calls=%fused_computation | loop fusion | flops 6289408 | bytes 4202496 | tf_op jit(solution)/shard_map/reduce_sum | solution.py:184
  30.3 3.7 %multiply_cosine_fusion = (f32[16,128,64]{2,1,0:T(8,128)S(1)}, f32[16,128,64]{2,1,0:T(8,128)S(1)}) fusion(f32[64]{0:T(128)S(1)} %negate_power_fusion, f32[16,128]{1,0:T(8,128)S(1)} %add_convert_fusion), kind=kLoop, calls=%fused_computation.5 | loop fusion | flops 131072 | bytes 1057024 | tf_op jit(solution)/shard_map/cos | solution.py:193
  34.4 2.3 %multiply_convert_fusion.scaled_ref = bf16[16,80,1024]{2,1,0:T(8,128)(2,1)} fusion(bf16[16,128,1024]{2,1,0:T(8,128)(2,1)S(1)} %bitcast.46, f32[1024]{0:T(1024)S(1)} %convert_element_type.36), kind=kLoop, calls=%fused_computation.1 | loop fusion | flops 3932160 | bytes 5246976 | tf_op jit(solution)/shard_map/convert_element_type | solution.py:181
  36.7 1.1 pad_maximum_fusion.turn_ref
  37.8 1.5 collective-permute-start.4
  39.3 2.7 %collective-permute-start.5 = (f32[16,128]{1,0:T(8,128)S(1)}, f32[16,128]{1,0:T(8,128)S(1)}, u32[]{:S(2)}, u32[]{:S(2)}) collective-permute-start(f32[16,128]{1,0:T(8,128)S(1)} %bitcast_add_fusion), channel_id=1, source_target_pairs={{0,4},{2,6},{4,0},{6,2},{1,5},{3,7},{5,1},{7,3},{8,12},{10,14},{12... | collective-permute-start | bytes 24584 | tf_op jit(solution)/shard_map/ppermute | solution.py:29
  42.0 1.4 collective-permute-start.6
  43.7 0.8 collective-permute-done.5
  44.5 1.2 collective-permute-done.6
  46.3 29.4 %all-gather.2.cloned.1.call-done.weight_ref = bf16[8,256,1024]{2,1,0:T(8,128)(2,1)} async-done(((bf16[1,256,1024]{2,1,0:T(8,128)(2,1)}), bf16[8,256,1024]{2,1,0:T(8,128)(2,1)}) %all-gather.2.cloned.1.call-update) | async-done | bytes 4194320 | tf_op jit(solution)/shard_map/all_gather | solution.py:54
  75.7 2.2 %copy-done.1 = bf16[8,256,1024]{2,1,0:T(8,128)(2,1)S(1)} copy-done((bf16[8,256,1024]{2,1,0:T(8,128)(2,1)S(1)}, bf16[8,256,1024]{2,1,0:T(8,128)(2,1)}, u32[]{:S(2)}) %copy-start.1) | copy-done | bytes 4194328
  77.9 2.4 %shard_map.113 = bf16[4,768,256]{2,1,0:T(8,128)(2,1)S(1)} custom-call(s32[2]{0:T(128)S(1)} %pad_add_fusion.1.place_ref, bf16[16,48,1024]{2,1,0:T(8,128)(2,1)S(1)} %multiply_convert_fusion.1.scaled_ref, bf16[8,256,1024]{2,1,0:T(8,128)(2,1)S(1)} %copy-done.1), custom_call_target="tpu_custom_call" | custom-call | flops 1610612736 | bytes 5242880 | tf_op jit(solution)/shard_map/pallas_call | solution.py:87
  80.5 3.3 %collective-permute-done.7.refs_0_ = bf16[4,768,256]{2,1,0:T(8,128)(2,1)S(1)} collective-permute-done((bf16[4,768,256]{2,1,0:T(8,128)(2,1)S(1)}, bf16[4,768,256]{2,1,0:T(8,128)(2,1)S(1)}, u32[]{:S(2)}, u32[]{:S(2)}) %collective-permute-start.7) | collective-permute-done | bytes 1572896 | tf_op jit(solution)/shard_map/ppermute | solution.py:29
  83.8 3.2 %shard_map.114 = (bf16[768,256]{1,0:T(8,128)(2,1)S(1)}, bf16[768,256]{1,0:T(8,128)(2,1)}, bf16[768,256]{1,0:T(8,128)(2,1)}, bf16[768,256]{1,0:T(8,128)(2,1)}) custom-call(s32[2]{0:T(128)S(1)} %pad_add_fusion.place_ref, bf16[16,48,1024]{2,1,0:T(8,128)(2,1)S(1)} %multiply_convert_fusion.1.scaled_ref, bf16[8,256,1024]{2,1,0:T(8,128)(2,1)S(1)} %copy-done.1, ...), custom_call_target="tpu_custom_call" | custom-call | flops 1610612736 | bytes 5242880 | tf_op jit(solution)/shard_map/pallas_call | solution.py:87
  87.0 0.7 copy-done.6
  87.8 4.9 %shard_map.116 = bf16[4,1280,256]{2,1,0:T(8,128)(2,1)} custom-call(s32[2]{0:T(128)S(1)} %pad_add_fusion.1.place_ref, bf16[16,80,1024]{2,1,0:T(8,128)(2,1)S(1)} %copy-done.3, bf16[8,256,1024]{2,1,0:T(8,128)(2,1)S(1)} %copy-done.1), custom_call_target="tpu_custom_call" | custom-call | flops 2684354560 | bytes 7340032 | tf_op jit(solution)/shard_map/pallas_call | solution.py:87
  92.8 1.5 collective-permute-start.8
  94.3 2.7 %collective-permute-start.9 = (bf16[768,256]{1,0:T(8,128)(2,1)}, bf16[768,256]{1,0:T(8,128)(2,1)}, u32[]{:S(2)}, u32[]{:S(2)}) collective-permute-start(bf16[768,256]{1,0:T(8,128)(2,1)} %get-tuple-element.42), channel_id=1, source_target_pairs={{0,4},{2,6},{4,0},{6,2},{1,5},{3,7},{5,1},{7,3},{8,12},{10,14},{12... | collective-permute-start | bytes 1179656 | tf_op jit(solution)/shard_map/ppermute | solution.py:29
  97.0 1.5 collective-permute-start.10
  98.5 0.7 slice.25
  99.2 2.2 %copy-done.2 = bf16[8,256,1024]{2,1,0:T(8,128)(2,1)S(1)} copy-done((bf16[8,256,1024]{2,1,0:T(8,128)(2,1)S(1)}, bf16[8,256,1024]{2,1,0:T(8,128)(2,1)}, u32[]{:S(2)}) %copy-start.2) | copy-done | bytes 4194328
  101.4 5.8 %shard_map.117 = (bf16[1280,256]{1,0:T(8,128)(2,1)S(1)}, bf16[1280,256]{1,0:T(8,128)(2,1)}, bf16[1280,256]{1,0:T(8,128)(2,1)}, bf16[1280,256]{1,0:T(8,128)(2,1)}) custom-call(s32[2]{0:T(128)S(1)} %pad_add_fusion.place_ref, bf16[16,80,1024]{2,1,0:T(8,128)(2,1)S(1)} %copy-done.4, bf16[8,256,1024]{2,1,0:T(8,128)(2,1)S(1)} %copy-done.2, ...), custom_call_target="tpu_custom_call" | custom-call | flops 2684354560 | bytes 7340032 | tf_op jit(solution)/shard_map/pallas_call | solution.py:87
  107.8 2.3 %collective-permute-start.13 = (bf16[1280,256]{1,0:T(8,128)(2,1)}, bf16[1280,256]{1,0:T(8,128)(2,1)S(1)}, u32[]{:S(2)}, u32[]{:S(2)}) collective-permute-start(bf16[1280,256]{1,0:T(8,128)(2,1)} %get-tuple-element.49), channel_id=1, source_target_pairs={{0,4},{2,6},{4,0},{6,2},{1,5},{3,7},{5,1},{7,3},{8,12},{10,14},{12... | collective-permute-start | bytes 1966088 | tf_op jit(solution)/shard_map/ppermute | solution.py:29
  110.1 1.5 collective-permute-start.14
  111.6 4.1 %collective-permute-done.9 = bf16[768,256]{1,0:T(8,128)(2,1)} collective-permute-done((bf16[768,256]{1,0:T(8,128)(2,1)}, bf16[768,256]{1,0:T(8,128)(2,1)}, u32[]{:S(2)}, u32[]{:S(2)}) %collective-permute-start.9) | collective-permute-done | bytes 393248 | tf_op jit(solution)/shard_map/ppermute | solution.py:29
  115.9 3.7 %shard_map.115 = bf16[32,48,256]{2,1,0:T(8,128)(2,1)} custom-call(s32[16]{0:T(128)S(1)} %multiply_add_fusion.target_ref, s32[16]{0:T(128)S(1)} %copy-done.8, f32[16,48,128]{2,1,0:T(8,128)S(1)} %broadcast_in_dim.16.inverse_ref, f32[16,48,128]{2,1,0:T(8,128)S(1)} %pad_maximum_fusion.1.turn_ref, bf16[1,256]{1,0:T(2,128)(2,1)S(1)} %broadcast_in_dim.17.bias_ref, ...), custom_call_target="tpu_custom_call" | custom-call | flops 40000000000 | bytes 3145728 | tf_op jit(solution)/shard_map/pallas_call | solution.py:129
  119.9 8.9 %all-to-all-start = ((bf16[32,48,256]{2,1,0:T(8,128)(2,1)}), bf16[32,48,256]{2,1,0:T(8,128)(2,1)}, u32[]{:S(2)}, u32[]{:S(2)}) async-start(bf16[32,48,256]{2,1,0:T(8,128)(2,1)} %shard_map.115), calls=%async_computation | async-start | bytes 1572864 | tf_op jit(solution)/shard_map/all_to_all | solution.py:235
  128.8 0.8 collective-permute-done.12
  129.6 13.6 %collective-permute-done.13 = bf16[1280,256]{1,0:T(8,128)(2,1)S(1)} collective-permute-done((bf16[1280,256]{1,0:T(8,128)(2,1)}, bf16[1280,256]{1,0:T(8,128)(2,1)S(1)}, u32[]{:S(2)}, u32[]{:S(2)}) %collective-permute-start.13) | collective-permute-done | bytes 655392 | tf_op jit(solution)/shard_map/ppermute | solution.py:29
  143.1 1.1 copy-done.10
  144.2 3.9 %shard_map.118 = bf16[32,80,256]{2,1,0:T(8,128)(2,1)} custom-call(s32[16]{0:T(128)S(1)} %multiply_add_fusion.target_ref, s32[16]{0:T(128)S(1)} %copy-done.8, f32[16,80,128]{2,1,0:T(8,128)S(1)} %broadcast_in_dim.18.inverse_ref, f32[16,80,128]{2,1,0:T(8,128)S(1)} %copy-done.5, bf16[1,256]{1,0:T(2,128)(2,1)S(1)} %broadcast_in_dim.17.bias_ref, ...), custom_call_target="tpu_custom_call" | custom-call | flops 40000000000 | bytes 5242880 | tf_op jit(solution)/shard_map/pallas_call | solution.py:129
  148.2 1.2 all-to-all-done
  149.4 7.9 %all-to-all-start.1 = ((bf16[32,80,256]{2,1,0:T(8,128)(2,1)}), bf16[32,80,256]{2,1,0:T(8,128)(2,1)S(1)}, u32[]{:S(2)}, u32[]{:S(2)}) async-start(bf16[32,80,256]{2,1,0:T(8,128)(2,1)} %shard_map.118), calls=%async_computation.3 | async-start | bytes 2621440 | tf_op jit(solution)/shard_map/all_to_all | solution.py:235
  157.3 0.7 convert_element_type.44
  158.0 2.1 %constant_dynamic-update-slice_fusion.1 = bf16[32,128,256]{2,1,0:T(8,128)(2,1)} fusion(bf16[32,128,256]{2,1,0:T(8,128)(2,1)} %shard_map.112, bf16[32,48,256]{2,1,0:T(8,128)(2,1)} %all-to-all-done), kind=kLoop, calls=%fused_computation.22 | loop fusion | bytes 1572864 | tf_op jit(solution)/shard_map/dynamic_update_slice | solution.py:236
  160.1 4.2 %convolution_convert_fusion.1 = bf16[256,1024]{1,0:T(8,128)(2,1)} fusion(bf16[256,2048]{1,0:T(8,128)(2,1)S(1)} %copy-done.13, bf16[2048,1024]{1,0:T(8,128)(2,1)} %bitcast.40), kind=kOutput, calls=%fused_computation.6 | convolution fusion | flops 1074003968 | bytes 5767168 | tf_op jit(solution)/shard_map/dot_general | solution.py:239
  164.3 23.9 %all-to-all-done.1 = bf16[32,80,256]{2,1,0:T(8,128)(2,1)S(1)} async-done(((bf16[32,80,256]{2,1,0:T(8,128)(2,1)}), bf16[32,80,256]{2,1,0:T(8,128)(2,1)S(1)}, u32[]{:S(2)}, u32[]{:S(2)}) %all-to-all-start.1) | async-done | bytes 1310752 | tf_op jit(solution)/shard_map/all_to_all | solution.py:235
  188.2 1.1 constant_dynamic-update-slice_fusion
  (81 shorter events, 3.8 us)
Async XLA Ops:
  8.0 15.1 %copy-start = (bf16[256,1024]{1,0:T(8,128)(2,1)S(1)}, bf16[256,1024]{1,0:T(8,128)(2,1)}, u32[]{:S(2)}) copy-start(bf16[256,1024]{1,0:T(8,128)(2,1)} %param.16) | copy-start | bytes 1572868
  8.0 14.5 %copy-start.12 = (bf16[256,2048]{1,0:T(8,128)(2,1)S(1)}, bf16[256,2048]{1,0:T(8,128)(2,1)}, u32[]{:S(2)}) copy-start(bf16[256,2048]{1,0:T(8,128)(2,1)} %param.17) | copy-start | bytes 3145732
  8.0 67.7 %all-gather.2.cloned.1.call-start = ((), (), s32[]{:S(2)}) async-start(), calls=%async_computation.4 | async-start | bytes 4718592 | tf_op jit(solution)/shard_map/all_gather | solution.py:54
  8.1 9.0 %collective-permute-start = (bf16[64,1024]{1,0:T(8,128)(2,1)}, bf16[64,1024]{1,0:T(8,128)(2,1)S(1)}, u32[]{:S(2)}, u32[]{:S(2)}) collective-permute-start(bf16[64,1024]{1,0:T(8,128)(2,1)} %param.9), channel_id=1, source_target_pairs={{0,24},{8,0},{16,8},{24,16},{1,25},{9,1},{17,9},{25,17},{2,26},{10... | collective-permute-start | bytes 393224 | tf_op jit(solution)/shard_map/ppermute | solution.py:29
  11.2 8.1 %collective-permute-start.1 = (bf16[64,1024]{1,0:T(8,128)(2,1)}, bf16[64,1024]{1,0:T(8,128)(2,1)S(1)}, u32[]{:S(2)}, u32[]{:S(2)}) collective-permute-start(bf16[64,1024]{1,0:T(8,128)(2,1)} %param.9), channel_id=1, source_target_pairs={{0,16},{8,24},{16,0},{24,8},{1,17},{9,25},{17,1},{25,9},{2,18},{10... | collective-permute-start | bytes 393224 | tf_op jit(solution)/shard_map/ppermute | solution.py:29
  11.8 8.8 %collective-permute-start.2 = (bf16[64,1024]{1,0:T(8,128)(2,1)}, bf16[64,1024]{1,0:T(8,128)(2,1)S(1)}, u32[]{:S(2)}, u32[]{:S(2)}) collective-permute-start(bf16[64,1024]{1,0:T(8,128)(2,1)} %param.9), channel_id=1, source_target_pairs={{0,8},{8,16},{16,24},{24,0},{1,9},{9,17},{17,25},{25,1},{2,10},{10... | collective-permute-start | bytes 393224 | tf_op jit(solution)/shard_map/ppermute | solution.py:29
  22.5 76.7 %reduce-scatter.3.cloned.1.call-start = ((), (), s32[]{:S(2)}) async-start(), calls=%async_computation.5 | async-start | bytes 5242880 | tf_op jit(solution)/shard_map/reduce_scatter | solution.py:173
  26.5 3.5 %copy-start.18 = (bf16[1024]{0:T(1024)(128)(2,1)S(1)}, bf16[1024]{0:T(1024)(128)(2,1)}, u32[]{:S(2)}) copy-start(bf16[1024]{0:T(1024)(128)(2,1)} %param.11) | copy-start | bytes 6148
  26.5 3.5 %copy-start.20 = (s32[16,1]{0,1:T(1,128)S(1)}, s32[16,1]{0,1:T(1,128)}, u32[]{:S(2)}) copy-start(s32[16,1]{0,1:T(1,128)} %param.13) | copy-start | bytes 196
  26.5 3.7 %copy-start.19 = (s32[16]{0:T(128)S(1)}, s32[16]{0:T(128)}, u32[]{:S(2)}) copy-start(s32[16]{0:T(128)} %param.14) | copy-start | bytes 196
  26.5 122.9 %reduce-scatter.5.cloned.1.call-start = ((), (), s32[]{:S(2)}) async-start(), calls=%async_computation.6 | async-start | bytes 1179648 | tf_op jit(solution)/shard_map/reduce_scatter | solution.py:208
  26.7 7.3 %copy-start.11 = (bf16[2048,1024]{1,0:T(8,128)(2,1)S(1)}, bf16[2048,1024]{1,0:T(8,128)(2,1)}, u32[]{:S(2)}) copy-start(bf16[2048,1024]{1,0:T(8,128)(2,1)} %param.12) | copy-start | bytes 12582916
  29.9 7.9 %collective-permute-start.3 = (f32[16,128]{1,0:T(8,128)S(1)}, f32[16,128]{1,0:T(8,128)S(1)}, u32[]{:S(2)}, u32[]{:S(2)}) collective-permute-start(f32[16,128]{1,0:T(8,128)S(1)} %bitcast.50), channel_id=1, source_target_pairs={{0,1},{1,0},{2,3},{3,2},{4,5},{5,4},{6,7},{7,6},{8,9},{9,8},{10,11... | collective-permute-start | bytes 24584 | tf_op jit(solution)/shard_map/ppermute | solution.py:29
  37.8 5.8 %collective-permute-start.4 = (f32[16,128]{1,0:T(8,128)S(1)}, f32[16,128]{1,0:T(8,128)S(1)}, u32[]{:S(2)}, u32[]{:S(2)}) collective-permute-start(f32[16,128]{1,0:T(8,128)S(1)} %bitcast_add_fusion), channel_id=1, source_target_pairs={{0,2},{2,4},{4,6},{6,0},{1,3},{3,5},{5,7},{7,1},{8,10},{10,12},{12... | collective-permute-start | bytes 24584 | tf_op jit(solution)/shard_map/ppermute | solution.py:29
  39.3 5.2 %collective-permute-start.5 = (f32[16,128]{1,0:T(8,128)S(1)}, f32[16,128]{1,0:T(8,128)S(1)}, u32[]{:S(2)}, u32[]{:S(2)}) collective-permute-start(f32[16,128]{1,0:T(8,128)S(1)} %bitcast_add_fusion), channel_id=1, source_target_pairs={{0,4},{2,6},{4,0},{6,2},{1,5},{3,7},{5,1},{7,3},{8,12},{10,14},{12... | collective-permute-start | bytes 24584 | tf_op jit(solution)/shard_map/ppermute | solution.py:29
  42.0 3.7 %collective-permute-start.6 = (f32[16,128]{1,0:T(8,128)S(1)}, f32[16,128]{1,0:T(8,128)S(1)}, u32[]{:S(2)}, u32[]{:S(2)}) collective-permute-start(f32[16,128]{1,0:T(8,128)S(1)} %bitcast_add_fusion), channel_id=1, source_target_pairs={{0,6},{2,0},{4,2},{6,4},{1,7},{3,1},{5,3},{7,5},{8,14},{10,8},{12,... | collective-permute-start | bytes 24584 | tf_op jit(solution)/shard_map/ppermute | solution.py:29
  75.7 2.2 %copy-start.1 = (bf16[8,256,1024]{2,1,0:T(8,128)(2,1)S(1)}, bf16[8,256,1024]{2,1,0:T(8,128)(2,1)}, u32[]{:S(2)}) copy-start(bf16[8,256,1024]{2,1,0:T(8,128)(2,1)} %all-gather.2.cloned.1.call-done.weight_ref) | copy-start | bytes 12582916
  80.3 3.5 %collective-permute-start.7 = (bf16[4,768,256]{2,1,0:T(8,128)(2,1)S(1)}, bf16[4,768,256]{2,1,0:T(8,128)(2,1)S(1)}, u32[]{:S(2)}, u32[]{:S(2)}) collective-permute-start(bf16[4,768,256]{2,1,0:T(8,128)(2,1)S(1)} %shard_map.113), channel_id=1, source_target_pairs={{0,1},{1,0},{2,3},{3,2},{4,5},{5,4},{6,7},{7,6},{8,9},{9,8},{10,11... | collective-permute-start | bytes 4718600 | tf_op jit(solution)/shard_map/ppermute | solution.py:29
  80.5 7.3 %copy-start.3 = (bf16[16,80,1024]{2,1,0:T(8,128)(2,1)S(1)}, bf16[16,80,1024]{2,1,0:T(8,128)(2,1)}, u32[]{:S(2)}) copy-start(bf16[16,80,1024]{2,1,0:T(8,128)(2,1)} %multiply_convert_fusion.scaled_ref) | copy-start | bytes 7864324
  87.0 0.8 copy-start.6
  87.8 10.7 %copy-start.21 = (bf16[256]{0:T(256)(128)(2,1)S(1)}, bf16[256]{0:T(256)(128)(2,1)}, u32[]{:S(2)}) copy-start(bf16[256]{0:T(256)(128)(2,1)} %param.10) | copy-start | bytes 1540
  87.8 10.7 %copy-start.15 = (f32[16,128]{1,0:T(8,128)S(1)}, f32[16,128]{1,0:T(8,128)}, u32[]{:S(2)}) copy-start(f32[16,128]{1,0:T(8,128)} %add_rsqrt_fusion) | copy-start | bytes 24580
  87.8 11.4 %copy-start.4 = (bf16[16,80,1024]{2,1,0:T(8,128)(2,1)S(1)}, bf16[16,80,1024]{2,1,0:T(8,128)(2,1)}, u32[]{:S(2)}) copy-start(bf16[16,80,1024]{2,1,0:T(8,128)(2,1)} %multiply_convert_fusion.scaled_ref) | copy-start | bytes 7864324
  92.7 6.5 %collective-permute-start.11 = (bf16[4,1280,256]{2,1,0:T(8,128)(2,1)}, bf16[4,1280,256]{2,1,0:T(8,128)(2,1)}, u32[]{:S(2)}, u32[]{:S(2)}) collective-permute-start(bf16[4,1280,256]{2,1,0:T(8,128)(2,1)} %shard_map.116), channel_id=1, source_target_pairs={{0,1},{1,0},{2,3},{3,2},{4,5},{5,4},{6,7},{7,6},{8,9},{9,8},{10,11... | collective-permute-start | bytes 7864328 | tf_op jit(solution)/shard_map/ppermute | solution.py:29
  92.8 17.3 %collective-permute-start.8 = (bf16[768,256]{1,0:T(8,128)(2,1)}, bf16[768,256]{1,0:T(8,128)(2,1)}, u32[]{:S(2)}, u32[]{:S(2)}) collective-permute-start(bf16[768,256]{1,0:T(8,128)(2,1)} %get-tuple-element.41), channel_id=1, source_target_pairs={{0,2},{2,4},{4,6},{6,0},{1,3},{3,5},{5,7},{7,1},{8,10},{10,12},{12... | collective-permute-start | bytes 1179656 | tf_op jit(solution)/shard_map/ppermute | solution.py:29
  94.3 21.4 %collective-permute-start.9 = (bf16[768,256]{1,0:T(8,128)(2,1)}, bf16[768,256]{1,0:T(8,128)(2,1)}, u32[]{:S(2)}, u32[]{:S(2)}) collective-permute-start(bf16[768,256]{1,0:T(8,128)(2,1)} %get-tuple-element.42), channel_id=1, source_target_pairs={{0,4},{2,6},{4,0},{6,2},{1,5},{3,7},{5,1},{7,3},{8,12},{10,14},{12... | collective-permute-start | bytes 1179656 | tf_op jit(solution)/shard_map/ppermute | solution.py:29
  97.0 18.7 %collective-permute-start.10 = (bf16[768,256]{1,0:T(8,128)(2,1)}, bf16[768,256]{1,0:T(8,128)(2,1)}, u32[]{:S(2)}, u32[]{:S(2)}) collective-permute-start(bf16[768,256]{1,0:T(8,128)(2,1)} %get-tuple-element.43), channel_id=1, source_target_pairs={{0,6},{2,0},{4,2},{6,4},{1,7},{3,1},{5,3},{7,5},{8,14},{10,8},{12,... | collective-permute-start | bytes 1179656 | tf_op jit(solution)/shard_map/ppermute | solution.py:29
  99.2 2.2 %copy-start.2 = (bf16[8,256,1024]{2,1,0:T(8,128)(2,1)S(1)}, bf16[8,256,1024]{2,1,0:T(8,128)(2,1)}, u32[]{:S(2)}) copy-start(bf16[8,256,1024]{2,1,0:T(8,128)(2,1)} %all-gather.2.cloned.1.call-done.weight_ref) | copy-start | bytes 12582916
  101.4 14.3 %copy-start.16 = (f32[16,128]{1,0:T(8,128)S(1)}, f32[16,128]{1,0:T(8,128)}, u32[]{:S(2)}) copy-start(f32[16,128]{1,0:T(8,128)} %add_rsqrt_fusion) | copy-start | bytes 24580
  101.4 14.5 %copy-start.7 = (bf16[768,256]{1,0:T(8,128)(2,1)S(1)}, bf16[768,256]{1,0:T(8,128)(2,1)}, u32[]{:S(2)}) copy-start(bf16[768,256]{1,0:T(8,128)(2,1)} %copy-done.6) | copy-start | bytes 1179652
  101.4 14.5 %copy-start.8 = (s32[16]{0:T(128)S(1)}, s32[16]{0:T(128)}, u32[]{:S(2)}) copy-start(s32[16]{0:T(128)} %fill_ref.3) | copy-start | bytes 196
  107.2 12.4 %copy-start.9 = (bf16[1280,256]{1,0:T(8,128)(2,1)}, bf16[1280,256]{1,0:T(8,128)(2,1)S(1)}, u32[]{:S(2)}) copy-start(bf16[1280,256]{1,0:T(8,128)(2,1)S(1)} %get-tuple-element.47) | copy-start | bytes 1966084
  107.2 22.4 %collective-permute-start.12 = (bf16[1280,256]{1,0:T(8,128)(2,1)}, bf16[1280,256]{1,0:T(8,128)(2,1)S(1)}, u32[]{:S(2)}, u32[]{:S(2)}) collective-permute-start(bf16[1280,256]{1,0:T(8,128)(2,1)} %get-tuple-element.48), channel_id=1, source_target_pairs={{0,2},{2,4},{4,6},{6,0},{1,3},{3,5},{5,7},{7,1},{8,10},{10,12},{12... | collective-permute-start | bytes 1966088 | tf_op jit(solution)/shard_map/ppermute | solution.py:29
  107.8 35.4 %collective-permute-start.13 = (bf16[1280,256]{1,0:T(8,128)(2,1)}, bf16[1280,256]{1,0:T(8,128)(2,1)S(1)}, u32[]{:S(2)}, u32[]{:S(2)}) collective-permute-start(bf16[1280,256]{1,0:T(8,128)(2,1)} %get-tuple-element.49), channel_id=1, source_target_pairs={{0,4},{2,6},{4,0},{6,2},{1,5},{3,7},{5,1},{7,3},{8,12},{10,14},{12... | collective-permute-start | bytes 1966088 | tf_op jit(solution)/shard_map/ppermute | solution.py:29
  110.1 33.0 %collective-permute-start.14 = (bf16[1280,256]{1,0:T(8,128)(2,1)}, bf16[1280,256]{1,0:T(8,128)(2,1)}, u32[]{:S(2)}, u32[]{:S(2)}) collective-permute-start(bf16[1280,256]{1,0:T(8,128)(2,1)} %get-tuple-element.50), channel_id=1, source_target_pairs={{0,6},{2,0},{4,2},{6,4},{1,7},{3,1},{5,3},{7,5},{8,14},{10,8},{12,... | collective-permute-start | bytes 1966088 | tf_op jit(solution)/shard_map/ppermute | solution.py:29
  115.9 3.7 %copy-start.17 = (f32[16,80]{1,0:T(8,128)S(1)}, f32[16,80]{1,0:T(8,128)}, u32[]{:S(2)}) copy-start(f32[16,80]{1,0:T(8,128)} %slice.25) | copy-start | bytes 15364
  115.9 27.2 %copy-start.5 = (f32[16,80,128]{2,1,0:T(8,128)S(1)}, f32[16,80,128]{2,1,0:T(8,128)}, u32[]{:S(2)}) copy-start(f32[16,80,128]{2,1,0:T(8,128)} %pad_maximum_fusion.turn_ref) | copy-start | bytes 1966084
  119.9 29.5 %all-to-all-start = ((bf16[32,48,256]{2,1,0:T(8,128)(2,1)}), bf16[32,48,256]{2,1,0:T(8,128)(2,1)}, u32[]{:S(2)}, u32[]{:S(2)}) async-start(bf16[32,48,256]{2,1,0:T(8,128)(2,1)} %shard_map.115), calls=%async_computation | async-start | bytes 1572864 | tf_op jit(solution)/shard_map/all_to_all | solution.py:235
  143.1 1.1 copy-start.10
  149.4 7.9 %copy-start.14 = (bf16[64,1024]{1,0:T(8,128)(2,1)S(1)}, bf16[64,1024]{1,0:T(8,128)(2,1)}, u32[]{:S(2)}) copy-start(bf16[64,1024]{1,0:T(8,128)(2,1)} %reduce-scatter.5.cloned.1.call-done) | copy-start | bytes 393220
  149.4 38.9 %all-to-all-start.1 = ((bf16[32,80,256]{2,1,0:T(8,128)(2,1)}), bf16[32,80,256]{2,1,0:T(8,128)(2,1)S(1)}, u32[]{:S(2)}, u32[]{:S(2)}) async-start(bf16[32,80,256]{2,1,0:T(8,128)(2,1)} %shard_map.118), calls=%async_computation.3 | async-start | bytes 2621440 | tf_op jit(solution)/shard_map/all_to_all | solution.py:235
  157.3 2.8 %copy-start.13 = (bf16[256,2048]{1,0:T(8,128)(2,1)S(1)}, bf16[256,2048]{1,0:T(8,128)(2,1)}, u32[]{:S(2)}) copy-start(bf16[256,2048]{1,0:T(8,128)(2,1)} %param.17) | copy-start | bytes 3145732
Sparse Core Ops, SparseCore 0:
  22.6 53.0 all-gather.1
  99.3 40.2 reduce-scatter.4
Sparse Core Ops, SparseCore 1:
  26.6 49.3 reduce-scatter.2

commit v4 on v3

--- a/solution.py
+++ b/solution.py
@@ -227,7 +227,7 @@
             parts, inverse[c], turn[c], kv_bias[None, :], target, page_fill, start, slots
         )
         if c == 0:
-            placed = after(placed, mine[len(CHUNKS) - 1], inverse[1:])
+            placed = after(placed, inverse[1:])
         else:
             placed = after(placed, piece)
         if c == len(CHUNKS) - 1:

time: 197 us -> 197 us (level)
  no operation moved by 1% of the time
where the time goes in v4:
time: 197 us
  waiting for transfers between devices  85.3 us (43%)
  starting transfers between devices  37.6 us (19%)
  Pallas kernels  24 us (12%)
  between operations  15.8 us (8%)
  local copies, waits for them, and re-layouts  13.9 us (7%)
  other arithmetic  12.7 us (6%)
  matrix products  7.53 us (4%)
    ppermute x15, waiting for transfers between devices, shift(): return lax.ppermute(value, axis, ring(size, step))  30.7 us
    all_gather x1, waiting for transfers between devices, gather_weight(): return (lax.all_gather(line, Z, axis=0, tiled=False), line)  29.4 us
    all_to_all x2, waiting for transfers between devices, shards(): piece = lax.all_to_all(placed, DP, 0, 0, tiled=True)  25.2 us
    ppermute x15, starting transfers between devices, shift(): return lax.ppermute(value, axis, ring(size, step))  20.7 us
    all_to_all x2, starting transfers between devices, shards(): piece = lax.all_to_all(placed, DP, 0, 0, tiled=True)  16.8 us
    pallas_call x4, Pallas kernels, project(): pl.pallas_call(kernel, in_specs=[SMEM] + [VMEM] * (len(args) - 1), out_sp...  16.3 us
    unnamed x50, local copies, waits for them, and re-layouts  8.2 us
    pallas_call x2, Pallas kernels, finish(): pl.pallas_call(kernel, in_specs=[SMEM, SMEM] + [VMEM] * (3 + len(parts)),...  7.63 us
  transfers between devices with their start and end apart: 20, of which 12 were waited for; matrix products, arithmetic and copies ran while one was open for 13% of the time, Pallas kernels for 12%

profile of v4, /device:TPU:32, one launch (start us, length us, event | category | flops | bytes accessed | tf_op | source)
XLA Modules:
  0.0 196.8 jit_solution(5696309410667952927)
XLA Ops:
  8.1 3.1 %collective-permute-start = (bf16[64,1024]{1,0:T(8,128)(2,1)}, bf16[64,1024]{1,0:T(8,128)(2,1)S(1)}, u32[]{:S(2)}, u32[]{:S(2)}) collective-permute-start(bf16[64,1024]{1,0:T(8,128)(2,1)} %param.9), channel_id=1, source_target_pairs={{0,24},{8,0},{16,8},{24,16},{1,25},{9,1},{17,9},{25,17},{2,26},{10... | collective-permute-start | bytes 393224 | tf_op jit(solution)/shard_map/ppermute | solution.py:29
  11.2 0.6 collective-permute-start.1
  11.8 1.0 collective-permute-start.2
  12.8 0.9 bitcast_dynamic-update-slice_fusion.5
  13.7 3.3 %collective-permute-done = bf16[64,1024]{1,0:T(8,128)(2,1)S(1)} collective-permute-done((bf16[64,1024]{1,0:T(8,128)(2,1)}, bf16[64,1024]{1,0:T(8,128)(2,1)S(1)}, u32[]{:S(2)}, u32[]{:S(2)}) %collective-permute-start) | collective-permute-done | bytes 131104 | tf_op jit(solution)/shard_map/ppermute | solution.py:29
  17.1 2.2 %collective-permute-done.1 = bf16[64,1024]{1,0:T(8,128)(2,1)S(1)} collective-permute-done((bf16[64,1024]{1,0:T(8,128)(2,1)}, bf16[64,1024]{1,0:T(8,128)(2,1)S(1)}, u32[]{:S(2)}, u32[]{:S(2)}) %collective-permute-start.1) | collective-permute-done | bytes 131104 | tf_op jit(solution)/shard_map/ppermute | solution.py:29
  19.3 1.4 collective-permute-done.2
  20.7 0.9 bitcast_dynamic-update-slice_fusion.6
  21.6 0.8 constant_dynamic-slice_fusion
  23.2 3.3 %convolution_convert_fusion = bf16[2048,1024]{1,0:T(8,128)(2,1)} fusion(bf16[256,2048]{0,1:T(8,128)(2,1)S(1)} %bitcast.47, bf16[256,1024]{1,0:T(8,128)(2,1)S(1)} %copy-done), kind=kOutput, calls=%fused_computation.2 | convolution fusion | flops 1075838976 | bytes 5767168 | tf_op jit(solution)/shard_map/dot_general | solution.py:170
  26.7 3.2 %multiply_reduce_fusion = f32[2048]{0:T(1024)S(1)} fusion(bf16[2048,1024]{1,0:T(8,128)(2,1)} %param.12), kind=kLoop, calls=%fused_computation | loop fusion | flops 6289408 | bytes 4202496 | tf_op jit(solution)/shard_map/reduce_sum | solution.py:184
  30.3 3.7 %multiply_cosine_fusion = (f32[16,128,64]{2,1,0:T(8,128)S(1)}, f32[16,128,64]{2,1,0:T(8,128)S(1)}) fusion(f32[64]{0:T(128)S(1)} %negate_power_fusion, f32[16,128]{1,0:T(8,128)S(1)} %add_convert_fusion), kind=kLoop, calls=%fused_computation.5 | loop fusion | flops 131072 | bytes 1057024 | tf_op jit(solution)/shard_map/cos | solution.py:193
  34.4 2.3 %multiply_convert_fusion.scaled_ref = bf16[16,80,1024]{2,1,0:T(8,128)(2,1)} fusion(bf16[16,128,1024]{2,1,0:T(8,128)(2,1)S(1)} %bitcast.46, f32[1024]{0:T(1024)S(1)} %convert_element_type.36), kind=kLoop, calls=%fused_computation.1 | loop fusion | flops 3932160 | bytes 5246976 | tf_op jit(solution)/shard_map/convert_element_type | solution.py:181
  36.7 1.1 pad_maximum_fusion.turn_ref
  37.8 1.5 collective-permute-start.4
  39.3 2.7 %collective-permute-start.5 = (f32[16,128]{1,0:T(8,128)S(1)}, f32[16,128]{1,0:T(8,128)S(1)}, u32[]{:S(2)}, u32[]{:S(2)}) collective-permute-start(f32[16,128]{1,0:T(8,128)S(1)} %bitcast_add_fusion), channel_id=1, source_target_pairs={{0,4},{2,6},{4,0},{6,2},{1,5},{3,7},{5,1},{7,3},{8,12},{10,14},{12... | collective-permute-start | bytes 24584 | tf_op jit(solution)/shard_map/ppermute | solution.py:29
  42.0 1.4 collective-permute-start.6
  43.7 0.8 collective-permute-done.5
  44.5 1.2 collective-permute-done.6
  46.3 29.4 %all-gather.2.cloned.1.call-done.weight_ref = bf16[8,256,1024]{2,1,0:T(8,128)(2,1)} async-done(((bf16[1,256,1024]{2,1,0:T(8,128)(2,1)}), bf16[8,256,1024]{2,1,0:T(8,128)(2,1)}) %all-gather.2.cloned.1.call-update) | async-done | bytes 4194320 | tf_op jit(solution)/shard_map/all_gather | solution.py:54
  75.7 2.2 %copy-done.1 = bf16[8,256,1024]{2,1,0:T(8,128)(2,1)S(1)} copy-done((bf16[8,256,1024]{2,1,0:T(8,128)(2,1)S(1)}, bf16[8,256,1024]{2,1,0:T(8,128)(2,1)}, u32[]{:S(2)}) %copy-start.1) | copy-done | bytes 4194328
  77.9 2.4 %shard_map.113 = bf16[4,768,256]{2,1,0:T(8,128)(2,1)S(1)} custom-call(s32[2]{0:T(128)S(1)} %pad_add_fusion.1.place_ref, bf16[16,48,1024]{2,1,0:T(8,128)(2,1)S(1)} %multiply_convert_fusion.1.scaled_ref, bf16[8,256,1024]{2,1,0:T(8,128)(2,1)S(1)} %copy-done.1), custom_call_target="tpu_custom_call" | custom-call | flops 1610612736 | bytes 5242880 | tf_op jit(solution)/shard_map/pallas_call | solution.py:87
  80.5 3.3 %collective-permute-done.7.refs_0_ = bf16[4,768,256]{2,1,0:T(8,128)(2,1)S(1)} collective-permute-done((bf16[4,768,256]{2,1,0:T(8,128)(2,1)S(1)}, bf16[4,768,256]{2,1,0:T(8,128)(2,1)S(1)}, u32[]{:S(2)}, u32[]{:S(2)}) %collective-permute-start.7) | collective-permute-done | bytes 1572896 | tf_op jit(solution)/shard_map/ppermute | solution.py:29
  83.8 3.2 %shard_map.114 = (bf16[768,256]{1,0:T(8,128)(2,1)S(1)}, bf16[768,256]{1,0:T(8,128)(2,1)}, bf16[768,256]{1,0:T(8,128)(2,1)}, bf16[768,256]{1,0:T(8,128)(2,1)}) custom-call(s32[2]{0:T(128)S(1)} %pad_add_fusion.place_ref, bf16[16,48,1024]{2,1,0:T(8,128)(2,1)S(1)} %multiply_convert_fusion.1.scaled_ref, bf16[8,256,1024]{2,1,0:T(8,128)(2,1)S(1)} %copy-done.1, ...), custom_call_target="tpu_custom_call" | custom-call | flops 1610612736 | bytes 5242880 | tf_op jit(solution)/shard_map/pallas_call | solution.py:87
  87.0 0.7 copy-done.6
  87.8 4.9 %shard_map.116 = bf16[4,1280,256]{2,1,0:T(8,128)(2,1)} custom-call(s32[2]{0:T(128)S(1)} %pad_add_fusion.1.place_ref, bf16[16,80,1024]{2,1,0:T(8,128)(2,1)S(1)} %copy-done.3, bf16[8,256,1024]{2,1,0:T(8,128)(2,1)S(1)} %copy-done.1), custom_call_target="tpu_custom_call" | custom-call | flops 2684354560 | bytes 7340032 | tf_op jit(solution)/shard_map/pallas_call | solution.py:87
  92.8 1.5 collective-permute-start.8
  94.3 2.7 %collective-permute-start.9 = (bf16[768,256]{1,0:T(8,128)(2,1)}, bf16[768,256]{1,0:T(8,128)(2,1)}, u32[]{:S(2)}, u32[]{:S(2)}) collective-permute-start(bf16[768,256]{1,0:T(8,128)(2,1)} %get-tuple-element.42), channel_id=1, source_target_pairs={{0,4},{2,6},{4,0},{6,2},{1,5},{3,7},{5,1},{7,3},{8,12},{10,14},{12... | collective-permute-start | bytes 1179656 | tf_op jit(solution)/shard_map/ppermute | solution.py:29
  97.0 1.5 collective-permute-start.10
  98.5 0.7 slice.25
  99.2 2.2 %copy-done.2 = bf16[8,256,1024]{2,1,0:T(8,128)(2,1)S(1)} copy-done((bf16[8,256,1024]{2,1,0:T(8,128)(2,1)S(1)}, bf16[8,256,1024]{2,1,0:T(8,128)(2,1)}, u32[]{:S(2)}) %copy-start.2) | copy-done | bytes 4194328
  101.4 5.8 %shard_map.117 = (bf16[1280,256]{1,0:T(8,128)(2,1)S(1)}, bf16[1280,256]{1,0:T(8,128)(2,1)}, bf16[1280,256]{1,0:T(8,128)(2,1)}, bf16[1280,256]{1,0:T(8,128)(2,1)}) custom-call(s32[2]{0:T(128)S(1)} %pad_add_fusion.place_ref, bf16[16,80,1024]{2,1,0:T(8,128)(2,1)S(1)} %copy-done.4, bf16[8,256,1024]{2,1,0:T(8,128)(2,1)S(1)} %copy-done.2, ...), custom_call_target="tpu_custom_call" | custom-call | flops 2684354560 | bytes 7340032 | tf_op jit(solution)/shard_map/pallas_call | solution.py:87
  107.8 2.3 %collective-permute-start.13 = (bf16[1280,256]{1,0:T(8,128)(2,1)}, bf16[1280,256]{1,0:T(8,128)(2,1)S(1)}, u32[]{:S(2)}, u32[]{:S(2)}) collective-permute-start(bf16[1280,256]{1,0:T(8,128)(2,1)} %get-tuple-element.51), channel_id=1, source_target_pairs={{0,4},{2,6},{4,0},{6,2},{1,5},{3,7},{5,1},{7,3},{8,12},{10,14},{12... | collective-permute-start | bytes 1966088 | tf_op jit(solution)/shard_map/ppermute | solution.py:29
  110.1 1.5 collective-permute-start.14
  111.6 4.1 %collective-permute-done.9 = bf16[768,256]{1,0:T(8,128)(2,1)} collective-permute-done((bf16[768,256]{1,0:T(8,128)(2,1)}, bf16[768,256]{1,0:T(8,128)(2,1)}, u32[]{:S(2)}, u32[]{:S(2)}) %collective-permute-start.9) | collective-permute-done | bytes 393248 | tf_op jit(solution)/shard_map/ppermute | solution.py:29
  115.9 3.7 %shard_map.115 = bf16[32,48,256]{2,1,0:T(8,128)(2,1)} custom-call(s32[16]{0:T(128)S(1)} %multiply_add_fusion.target_ref, s32[16]{0:T(128)S(1)} %copy-done.8, f32[16,48,128]{2,1,0:T(8,128)S(1)} %broadcast_in_dim.16.inverse_ref, f32[16,48,128]{2,1,0:T(8,128)S(1)} %pad_maximum_fusion.1.turn_ref, bf16[1,256]{1,0:T(2,128)(2,1)S(1)} %broadcast_in_dim.17.bias_ref, ...), custom_call_target="tpu_custom_call" | custom-call | flops 40000000000 | bytes 3145728 | tf_op jit(solution)/shard_map/pallas_call | solution.py:129
  119.9 8.9 %all-to-all-start = ((bf16[32,48,256]{2,1,0:T(8,128)(2,1)}), bf16[32,48,256]{2,1,0:T(8,128)(2,1)}, u32[]{:S(2)}, u32[]{:S(2)}) async-start(bf16[32,48,256]{2,1,0:T(8,128)(2,1)} %shard_map.115), calls=%async_computation | async-start | bytes 1572864 | tf_op jit(solution)/shard_map/all_to_all | solution.py:235
  128.8 0.8 collective-permute-done.12
  129.6 13.6 %collective-permute-done.13 = bf16[1280,256]{1,0:T(8,128)(2,1)S(1)} collective-permute-done((bf16[1280,256]{1,0:T(8,128)(2,1)}, bf16[1280,256]{1,0:T(8,128)(2,1)S(1)}, u32[]{:S(2)}, u32[]{:S(2)}) %collective-permute-start.13) | collective-permute-done | bytes 655392 | tf_op jit(solution)/shard_map/ppermute | solution.py:29
  143.1 1.1 copy-done.10
  144.2 3.9 %shard_map.118 = bf16[32,80,256]{2,1,0:T(8,128)(2,1)} custom-call(s32[16]{0:T(128)S(1)} %multiply_add_fusion.target_ref, s32[16]{0:T(128)S(1)} %copy-done.8, f32[16,80,128]{2,1,0:T(8,128)S(1)} %broadcast_in_dim.18.inverse_ref, f32[16,80,128]{2,1,0:T(8,128)S(1)} %copy-done.5, bf16[1,256]{1,0:T(2,128)(2,1)S(1)} %broadcast_in_dim.17.bias_ref, ...), custom_call_target="tpu_custom_call" | custom-call | flops 40000000000 | bytes 5242880 | tf_op jit(solution)/shard_map/pallas_call | solution.py:129
  148.2 1.2 all-to-all-done
  149.4 7.9 %all-to-all-start.1 = ((bf16[32,80,256]{2,1,0:T(8,128)(2,1)}), bf16[32,80,256]{2,1,0:T(8,128)(2,1)S(1)}, u32[]{:S(2)}, u32[]{:S(2)}) async-start(bf16[32,80,256]{2,1,0:T(8,128)(2,1)} %shard_map.118), calls=%async_computation.3 | async-start | bytes 2621440 | tf_op jit(solution)/shard_map/all_to_all | solution.py:235
  157.3 0.7 convert_element_type.44
  158.0 2.1 %constant_dynamic-update-slice_fusion.1 = bf16[32,128,256]{2,1,0:T(8,128)(2,1)} fusion(bf16[32,128,256]{2,1,0:T(8,128)(2,1)} %shard_map.112, bf16[32,48,256]{2,1,0:T(8,128)(2,1)} %all-to-all-done), kind=kLoop, calls=%fused_computation.22 | loop fusion | bytes 1572864 | tf_op jit(solution)/shard_map/dynamic_update_slice | solution.py:236
  160.1 4.2 %convolution_convert_fusion.1 = bf16[256,1024]{1,0:T(8,128)(2,1)} fusion(bf16[256,2048]{1,0:T(8,128)(2,1)S(1)} %copy-done.13, bf16[2048,1024]{1,0:T(8,128)(2,1)} %bitcast.40), kind=kOutput, calls=%fused_computation.6 | convolution fusion | flops 1074003968 | bytes 5767168 | tf_op jit(solution)/shard_map/dot_general | solution.py:239
  164.3 23.9 %all-to-all-done.1 = bf16[32,80,256]{2,1,0:T(8,128)(2,1)S(1)} async-done(((bf16[32,80,256]{2,1,0:T(8,128)(2,1)}), bf16[32,80,256]{2,1,0:T(8,128)(2,1)S(1)}, u32[]{:S(2)}, u32[]{:S(2)}) %all-to-all-start.1) | async-done | bytes 1310752 | tf_op jit(solution)/shard_map/all_to_all | solution.py:235
  188.2 1.1 constant_dynamic-update-slice_fusion
  (81 shorter events, 3.8 us)
Async XLA Ops:
  8.0 15.1 %copy-start = (bf16[256,1024]{1,0:T(8,128)(2,1)S(1)}, bf16[256,1024]{1,0:T(8,128)(2,1)}, u32[]{:S(2)}) copy-start(bf16[256,1024]{1,0:T(8,128)(2,1)} %param.16) | copy-start | bytes 1572868
  8.0 14.5 %copy-start.12 = (bf16[256,2048]{1,0:T(8,128)(2,1)S(1)}, bf16[256,2048]{1,0:T(8,128)(2,1)}, u32[]{:S(2)}) copy-start(bf16[256,2048]{1,0:T(8,128)(2,1)} %param.17) | copy-start | bytes 3145732
  8.0 67.7 %all-gather.2.cloned.1.call-start = ((), (), s32[]{:S(2)}) async-start(), calls=%async_computation.4 | async-start | bytes 4718592 | tf_op jit(solution)/shard_map/all_gather | solution.py:54
  8.1 9.0 %collective-permute-start = (bf16[64,1024]{1,0:T(8,128)(2,1)}, bf16[64,1024]{1,0:T(8,128)(2,1)S(1)}, u32[]{:S(2)}, u32[]{:S(2)}) collective-permute-start(bf16[64,1024]{1,0:T(8,128)(2,1)} %param.9), channel_id=1, source_target_pairs={{0,24},{8,0},{16,8},{24,16},{1,25},{9,1},{17,9},{25,17},{2,26},{10... | collective-permute-start | bytes 393224 | tf_op jit(solution)/shard_map/ppermute | solution.py:29
  11.2 8.1 %collective-permute-start.1 = (bf16[64,1024]{1,0:T(8,128)(2,1)}, bf16[64,1024]{1,0:T(8,128)(2,1)S(1)}, u32[]{:S(2)}, u32[]{:S(2)}) collective-permute-start(bf16[64,1024]{1,0:T(8,128)(2,1)} %param.9), channel_id=1, source_target_pairs={{0,16},{8,24},{16,0},{24,8},{1,17},{9,25},{17,1},{25,9},{2,18},{10... | collective-permute-start | bytes 393224 | tf_op jit(solution)/shard_map/ppermute | solution.py:29
  11.8 8.8 %collective-permute-start.2 = (bf16[64,1024]{1,0:T(8,128)(2,1)}, bf16[64,1024]{1,0:T(8,128)(2,1)S(1)}, u32[]{:S(2)}, u32[]{:S(2)}) collective-permute-start(bf16[64,1024]{1,0:T(8,128)(2,1)} %param.9), channel_id=1, source_target_pairs={{0,8},{8,16},{16,24},{24,0},{1,9},{9,17},{17,25},{25,1},{2,10},{10... | collective-permute-start | bytes 393224 | tf_op jit(solution)/shard_map/ppermute | solution.py:29
  22.5 76.7 %reduce-scatter.3.cloned.1.call-start = ((), (), s32[]{:S(2)}) async-start(), calls=%async_computation.5 | async-start | bytes 5242880 | tf_op jit(solution)/shard_map/reduce_scatter | solution.py:173
  26.5 3.5 %copy-start.18 = (bf16[1024]{0:T(1024)(128)(2,1)S(1)}, bf16[1024]{0:T(1024)(128)(2,1)}, u32[]{:S(2)}) copy-start(bf16[1024]{0:T(1024)(128)(2,1)} %param.11) | copy-start | bytes 6148
  26.5 3.5 %copy-start.20 = (s32[16,1]{0,1:T(1,128)S(1)}, s32[16,1]{0,1:T(1,128)}, u32[]{:S(2)}) copy-start(s32[16,1]{0,1:T(1,128)} %param.13) | copy-start | bytes 196
  26.5 3.7 %copy-start.19 = (s32[16]{0:T(128)S(1)}, s32[16]{0:T(128)}, u32[]{:S(2)}) copy-start(s32[16]{0:T(128)} %param.14) | copy-start | bytes 196
  26.5 122.9 %reduce-scatter.5.cloned.1.call-start = ((), (), s32[]{:S(2)}) async-start(), calls=%async_computation.6 | async-start | bytes 1179648 | tf_op jit(solution)/shard_map/reduce_scatter | solution.py:208
  26.7 7.3 %copy-start.11 = (bf16[2048,1024]{1,0:T(8,128)(2,1)S(1)}, bf16[2048,1024]{1,0:T(8,128)(2,1)}, u32[]{:S(2)}) copy-start(bf16[2048,1024]{1,0:T(8,128)(2,1)} %param.12) | copy-start | bytes 12582916
  29.9 7.9 %collective-permute-start.3 = (f32[16,128]{1,0:T(8,128)S(1)}, f32[16,128]{1,0:T(8,128)S(1)}, u32[]{:S(2)}, u32[]{:S(2)}) collective-permute-start(f32[16,128]{1,0:T(8,128)S(1)} %bitcast.50), channel_id=1, source_target_pairs={{0,1},{1,0},{2,3},{3,2},{4,5},{5,4},{6,7},{7,6},{8,9},{9,8},{10,11... | collective-permute-start | bytes 24584 | tf_op jit(solution)/shard_map/ppermute | solution.py:29
  37.8 5.8 %collective-permute-start.4 = (f32[16,128]{1,0:T(8,128)S(1)}, f32[16,128]{1,0:T(8,128)S(1)}, u32[]{:S(2)}, u32[]{:S(2)}) collective-permute-start(f32[16,128]{1,0:T(8,128)S(1)} %bitcast_add_fusion), channel_id=1, source_target_pairs={{0,2},{2,4},{4,6},{6,0},{1,3},{3,5},{5,7},{7,1},{8,10},{10,12},{12... | collective-permute-start | bytes 24584 | tf_op jit(solution)/shard_map/ppermute | solution.py:29
  39.3 5.2 %collective-permute-start.5 = (f32[16,128]{1,0:T(8,128)S(1)}, f32[16,128]{1,0:T(8,128)S(1)}, u32[]{:S(2)}, u32[]{:S(2)}) collective-permute-start(f32[16,128]{1,0:T(8,128)S(1)} %bitcast_add_fusion), channel_id=1, source_target_pairs={{0,4},{2,6},{4,0},{6,2},{1,5},{3,7},{5,1},{7,3},{8,12},{10,14},{12... | collective-permute-start | bytes 24584 | tf_op jit(solution)/shard_map/ppermute | solution.py:29
  42.0 3.7 %collective-permute-start.6 = (f32[16,128]{1,0:T(8,128)S(1)}, f32[16,128]{1,0:T(8,128)S(1)}, u32[]{:S(2)}, u32[]{:S(2)}) collective-permute-start(f32[16,128]{1,0:T(8,128)S(1)} %bitcast_add_fusion), channel_id=1, source_target_pairs={{0,6},{2,0},{4,2},{6,4},{1,7},{3,1},{5,3},{7,5},{8,14},{10,8},{12,... | collective-permute-start | bytes 24584 | tf_op jit(solution)/shard_map/ppermute | solution.py:29
  75.7 2.2 %copy-start.1 = (bf16[8,256,1024]{2,1,0:T(8,128)(2,1)S(1)}, bf16[8,256,1024]{2,1,0:T(8,128)(2,1)}, u32[]{:S(2)}) copy-start(bf16[8,256,1024]{2,1,0:T(8,128)(2,1)} %all-gather.2.cloned.1.call-done.weight_ref) | copy-start | bytes 12582916
  80.3 3.5 %collective-permute-start.7 = (bf16[4,768,256]{2,1,0:T(8,128)(2,1)S(1)}, bf16[4,768,256]{2,1,0:T(8,128)(2,1)S(1)}, u32[]{:S(2)}, u32[]{:S(2)}) collective-permute-start(bf16[4,768,256]{2,1,0:T(8,128)(2,1)S(1)} %shard_map.113), channel_id=1, source_target_pairs={{0,1},{1,0},{2,3},{3,2},{4,5},{5,4},{6,7},{7,6},{8,9},{9,8},{10,11... | collective-permute-start | bytes 4718600 | tf_op jit(solution)/shard_map/ppermute | solution.py:29
  80.5 7.3 %copy-start.3 = (bf16[16,80,1024]{2,1,0:T(8,128)(2,1)S(1)}, bf16[16,80,1024]{2,1,0:T(8,128)(2,1)}, u32[]{:S(2)}) copy-start(bf16[16,80,1024]{2,1,0:T(8,128)(2,1)} %multiply_convert_fusion.scaled_ref) | copy-start | bytes 7864324
  87.0 0.8 copy-start.6
  87.8 10.7 %copy-start.21 = (bf16[256]{0:T(256)(128)(2,1)S(1)}, bf16[256]{0:T(256)(128)(2,1)}, u32[]{:S(2)}) copy-start(bf16[256]{0:T(256)(128)(2,1)} %param.10) | copy-start | bytes 1540
  87.8 10.7 %copy-start.15 = (f32[16,128]{1,0:T(8,128)S(1)}, f32[16,128]{1,0:T(8,128)}, u32[]{:S(2)}) copy-start(f32[16,128]{1,0:T(8,128)} %add_rsqrt_fusion) | copy-start | bytes 24580
  87.8 11.4 %copy-start.4 = (bf16[16,80,1024]{2,1,0:T(8,128)(2,1)S(1)}, bf16[16,80,1024]{2,1,0:T(8,128)(2,1)}, u32[]{:S(2)}) copy-start(bf16[16,80,1024]{2,1,0:T(8,128)(2,1)} %multiply_convert_fusion.scaled_ref) | copy-start | bytes 7864324
  92.7 6.5 %collective-permute-start.11 = (bf16[4,1280,256]{2,1,0:T(8,128)(2,1)}, bf16[4,1280,256]{2,1,0:T(8,128)(2,1)}, u32[]{:S(2)}, u32[]{:S(2)}) collective-permute-start(bf16[4,1280,256]{2,1,0:T(8,128)(2,1)} %shard_map.116), channel_id=1, source_target_pairs={{0,1},{1,0},{2,3},{3,2},{4,5},{5,4},{6,7},{7,6},{8,9},{9,8},{10,11... | collective-permute-start | bytes 7864328 | tf_op jit(solution)/shard_map/ppermute | solution.py:29
  92.8 17.3 %collective-permute-start.8 = (bf16[768,256]{1,0:T(8,128)(2,1)}, bf16[768,256]{1,0:T(8,128)(2,1)}, u32[]{:S(2)}, u32[]{:S(2)}) collective-permute-start(bf16[768,256]{1,0:T(8,128)(2,1)} %get-tuple-element.41), channel_id=1, source_target_pairs={{0,2},{2,4},{4,6},{6,0},{1,3},{3,5},{5,7},{7,1},{8,10},{10,12},{12... | collective-permute-start | bytes 1179656 | tf_op jit(solution)/shard_map/ppermute | solution.py:29
  94.3 21.4 %collective-permute-start.9 = (bf16[768,256]{1,0:T(8,128)(2,1)}, bf16[768,256]{1,0:T(8,128)(2,1)}, u32[]{:S(2)}, u32[]{:S(2)}) collective-permute-start(bf16[768,256]{1,0:T(8,128)(2,1)} %get-tuple-element.42), channel_id=1, source_target_pairs={{0,4},{2,6},{4,0},{6,2},{1,5},{3,7},{5,1},{7,3},{8,12},{10,14},{12... | collective-permute-start | bytes 1179656 | tf_op jit(solution)/shard_map/ppermute | solution.py:29
  97.0 18.7 %collective-permute-start.10 = (bf16[768,256]{1,0:T(8,128)(2,1)}, bf16[768,256]{1,0:T(8,128)(2,1)}, u32[]{:S(2)}, u32[]{:S(2)}) collective-permute-start(bf16[768,256]{1,0:T(8,128)(2,1)} %get-tuple-element.43), channel_id=1, source_target_pairs={{0,6},{2,0},{4,2},{6,4},{1,7},{3,1},{5,3},{7,5},{8,14},{10,8},{12,... | collective-permute-start | bytes 1179656 | tf_op jit(solution)/shard_map/ppermute | solution.py:29
  99.2 2.2 %copy-start.2 = (bf16[8,256,1024]{2,1,0:T(8,128)(2,1)S(1)}, bf16[8,256,1024]{2,1,0:T(8,128)(2,1)}, u32[]{:S(2)}) copy-start(bf16[8,256,1024]{2,1,0:T(8,128)(2,1)} %all-gather.2.cloned.1.call-done.weight_ref) | copy-start | bytes 12582916
  101.4 14.3 %copy-start.16 = (f32[16,128]{1,0:T(8,128)S(1)}, f32[16,128]{1,0:T(8,128)}, u32[]{:S(2)}) copy-start(f32[16,128]{1,0:T(8,128)} %add_rsqrt_fusion) | copy-start | bytes 24580
  101.4 14.5 %copy-start.7 = (bf16[768,256]{1,0:T(8,128)(2,1)S(1)}, bf16[768,256]{1,0:T(8,128)(2,1)}, u32[]{:S(2)}) copy-start(bf16[768,256]{1,0:T(8,128)(2,1)} %copy-done.6) | copy-start | bytes 1179652
  101.4 14.5 %copy-start.8 = (s32[16]{0:T(128)S(1)}, s32[16]{0:T(128)}, u32[]{:S(2)}) copy-start(s32[16]{0:T(128)} %fill_ref.3) | copy-start | bytes 196
  107.2 12.4 %copy-start.9 = (bf16[1280,256]{1,0:T(8,128)(2,1)}, bf16[1280,256]{1,0:T(8,128)(2,1)S(1)}, u32[]{:S(2)}) copy-start(bf16[1280,256]{1,0:T(8,128)(2,1)S(1)} %get-tuple-element.49) | copy-start | bytes 1966084
  107.2 22.4 %collective-permute-start.12 = (bf16[1280,256]{1,0:T(8,128)(2,1)}, bf16[1280,256]{1,0:T(8,128)(2,1)S(1)}, u32[]{:S(2)}, u32[]{:S(2)}) collective-permute-start(bf16[1280,256]{1,0:T(8,128)(2,1)} %get-tuple-element.50), channel_id=1, source_target_pairs={{0,2},{2,4},{4,6},{6,0},{1,3},{3,5},{5,7},{7,1},{8,10},{10,12},{12... | collective-permute-start | bytes 1966088 | tf_op jit(solution)/shard_map/ppermute | solution.py:29
  107.8 35.4 %collective-permute-start.13 = (bf16[1280,256]{1,0:T(8,128)(2,1)}, bf16[1280,256]{1,0:T(8,128)(2,1)S(1)}, u32[]{:S(2)}, u32[]{:S(2)}) collective-permute-start(bf16[1280,256]{1,0:T(8,128)(2,1)} %get-tuple-element.51), channel_id=1, source_target_pairs={{0,4},{2,6},{4,0},{6,2},{1,5},{3,7},{5,1},{7,3},{8,12},{10,14},{12... | collective-permute-start | bytes 1966088 | tf_op jit(solution)/shard_map/ppermute | solution.py:29
  110.1 33.0 %collective-permute-start.14 = (bf16[1280,256]{1,0:T(8,128)(2,1)}, bf16[1280,256]{1,0:T(8,128)(2,1)}, u32[]{:S(2)}, u32[]{:S(2)}) collective-permute-start(bf16[1280,256]{1,0:T(8,128)(2,1)} %get-tuple-element.52), channel_id=1, source_target_pairs={{0,6},{2,0},{4,2},{6,4},{1,7},{3,1},{5,3},{7,5},{8,14},{10,8},{12,... | collective-permute-start | bytes 1966088 | tf_op jit(solution)/shard_map/ppermute | solution.py:29
  115.9 3.7 %copy-start.17 = (f32[16,80]{1,0:T(8,128)S(1)}, f32[16,80]{1,0:T(8,128)}, u32[]{:S(2)}) copy-start(f32[16,80]{1,0:T(8,128)} %slice.25) | copy-start | bytes 15364
  115.9 27.2 %copy-start.5 = (f32[16,80,128]{2,1,0:T(8,128)S(1)}, f32[16,80,128]{2,1,0:T(8,128)}, u32[]{:S(2)}) copy-start(f32[16,80,128]{2,1,0:T(8,128)} %pad_maximum_fusion.turn_ref) | copy-start | bytes 1966084
  119.9 29.5 %all-to-all-start = ((bf16[32,48,256]{2,1,0:T(8,128)(2,1)}), bf16[32,48,256]{2,1,0:T(8,128)(2,1)}, u32[]{:S(2)}, u32[]{:S(2)}) async-start(bf16[32,48,256]{2,1,0:T(8,128)(2,1)} %shard_map.115), calls=%async_computation | async-start | bytes 1572864 | tf_op jit(solution)/shard_map/all_to_all | solution.py:235
  143.1 1.1 copy-start.10
  149.4 7.9 %copy-start.14 = (bf16[64,1024]{1,0:T(8,128)(2,1)S(1)}, bf16[64,1024]{1,0:T(8,128)(2,1)}, u32[]{:S(2)}) copy-start(bf16[64,1024]{1,0:T(8,128)(2,1)} %reduce-scatter.5.cloned.1.call-done) | copy-start | bytes 393220
  149.4 38.9 %all-to-all-start.1 = ((bf16[32,80,256]{2,1,0:T(8,128)(2,1)}), bf16[32,80,256]{2,1,0:T(8,128)(2,1)S(1)}, u32[]{:S(2)}, u32[]{:S(2)}) async-start(bf16[32,80,256]{2,1,0:T(8,128)(2,1)} %shard_map.118), calls=%async_computation.3 | async-start | bytes 2621440 | tf_op jit(solution)/shard_map/all_to_all | solution.py:235
  157.3 2.8 %copy-start.13 = (bf16[256,2048]{1,0:T(8,128)(2,1)S(1)}, bf16[256,2048]{1,0:T(8,128)(2,1)}, u32[]{:S(2)}) copy-start(bf16[256,2048]{1,0:T(8,128)(2,1)} %param.17) | copy-start | bytes 3145732
Sparse Core Ops, SparseCore 0:
  22.6 53.0 all-gather.1
  99.3 40.2 reduce-scatter.4
Sparse Core Ops, SparseCore 1:
  26.6 49.3 reduce-scatter.2
